TPU v7x, 32 devices: a whole 2x2x4 slice. The times are simulated.
32 devices in a mesh: dev: 8 (over y, x, core), ta: 4 (over z).
Axes of the slice: x: 2, y: 2, z: 4, core: 2. Of those that a mesh axis runs over, the one named last changes fastest.
Arguments:
- tokens: bfloat16 [4, 16, 144, 384], P('ta', 'dev'), may hold values from -36 to 36
- out_grad: bfloat16 [4, 16, 144, 384], P('ta', 'dev'), may hold values from -6 to 6
- first_gain: float32 [384], replicated, may hold values from 0.25 to 1.75
- depth_qkv: bfloat16 [384, 1152], replicated, may hold values from -0.3125 to 0.3125
- depth_out: bfloat16 [384, 384], replicated, may hold values from -0.3125 to 0.3125
- time_qkv: bfloat16 [384, 1152], replicated, may hold values from -0.3125 to 0.3125
- time_out: bfloat16 [384, 384], replicated, may hold values from -0.3125 to 0.3125
- second_gain: float32 [384], replicated, may hold values from 0.25 to 1.75
- up_weight: bfloat16 [384, 1536], replicated, may hold values from -0.3125 to 0.3125
- spatial_kernel: float32 [3, 3, 3, 1536], replicated, may hold values from -1.25 to 1.25
- down_weight: bfloat16 [1536, 384], replicated, may hold values from -0.15625 to 0.15625
- depth_scale: float32 [6], replicated, may hold values from 2 to 10
- time_scale: float32 [6], replicated, may hold values from 2 to 10
Outputs:
- block_out: bfloat16 [4, 16, 144, 384], P('ta', 'dev')
- input_grad: bfloat16 [4, 16, 144, 384], P('ta', 'dev')
- depth_qkv_grad: float32 [384, 1152], replicated
- depth_out_grad: float32 [384, 384], replicated
- time_qkv_grad: float32 [384, 1152], replicated
- time_out_grad: float32 [384, 384], replicated
- up_grad: float32 [384, 1536], replicated
- kernel_grad: float32 [3, 3, 3, 1536], replicated
- down_grad: float32 [1536, 384], replicated
- first_gain_grad: float32 [384], replicated
- second_gain_grad: float32 [384], replicated
- depth_scale_grad: float32 [6], replicated
- time_scale_grad: float32 [6], replicated
All inputs are finite; a program needn't handle non-finite values.
Results may differ from a plain program's by a relative error of at most 0.015.
Values may be sent and summed in bfloat16 or wider, within the bound.
A program may use at most 128 MiB of HBM per device.

v0:
```python
import math

import jax
import jax.numpy as jnp
from jax import lax
from jax.sharding import PartitionSpec as P

PH = 6
PW = 24


def extended(block, sides, width):
    for axis, dim in sides:
        count = lax.axis_size(axis)
        forward = [(i, i + 1) for i in range(count - 1)]
        backward = [(target, source) for source, target in forward]
        low = lax.ppermute(
            lax.slice_in_dim(block, block.shape[dim] - width, None, axis=dim), axis, forward
        )
        high = lax.ppermute(lax.slice_in_dim(block, 0, width, axis=dim), axis, backward)
        block = jnp.concatenate([low, block, high], axis=dim)
    return block


def rounded(values):
    return lax.optimization_barrier(values.astype(jnp.bfloat16))


def normalize(values, gain):
    centered = values - jnp.mean(values, axis=-1, keepdims=True)
    spread = jnp.mean(centered * centered, axis=-1, keepdims=True)
    return centered * lax.rsqrt(spread + 1e-05) * gain


def project(left, weight):
    return jnp.dot(left, weight, preferred_element_type=jnp.float32)


def back_project(grads, weight):
    return lax.dot_general(
        grads, weight, (((grads.ndim - 1,), (1,)), ((), ())), preferred_element_type=jnp.float32
    )


def weight_grad(left, grads):
    lead = tuple(range(left.ndim - 1))
    return lax.dot_general(
        left, grads, ((lead, lead), ((), ())), preferred_element_type=jnp.float32
    )


def attend(fields, scale):
    width = fields.shape[-1] // 3
    heads = scale.shape[0]
    split_shape = fields.shape[:-1] + (heads, width // heads)
    query = fields[..., :width].reshape(split_shape)
    keyed = fields[..., width : 2 * width].reshape(split_shape)
    valued = fields[..., 2 * width :].reshape(split_shape)
    query = query * lax.rsqrt(jnp.sum(query * query, axis=-1, keepdims=True) + 1e-06)
    keyed = keyed * lax.rsqrt(jnp.sum(keyed * keyed, axis=-1, keepdims=True) + 1e-06)
    scores = jnp.einsum("plbhd,pmbhd->pbhlm", query, keyed, precision=lax.Precision.HIGHEST)
    scores = scores * scale[:, None, None]
    weights = jnp.exp(scores)
    weights = weights / jnp.sum(weights, axis=-1, keepdims=True)
    mixed = jnp.einsum("pbhlm,pmbhd->plbhd", weights, valued, precision=lax.Precision.HIGHEST)
    return mixed.reshape(fields.shape[:-1] + (width,))


def activate(values):
    return (
        0.5
        * values
        * (1.0 + jnp.tanh(0.7978845608 * (values + 0.044715 * values * values * values)))
    )


def filter_forward(padded, kernel):
    depth = padded.shape[1] - 2
    rows = padded.shape[2] - 2
    cols = padded.shape[3] - 2
    total = jnp.zeros((padded.shape[0], depth, rows, cols, padded.shape[4]), jnp.float32)
    for depth_off in range(3):
        for row_off in range(3):
            for col_off in range(3):
                window = padded[
                    :,
                    depth_off : depth_off + depth,
                    row_off : row_off + rows,
                    col_off : col_off + cols,
                ]
                total = total + kernel[depth_off, row_off, col_off] * window.astype(jnp.float32)
    return total


def filter_backward(grad_pad, kernel):
    depth = grad_pad.shape[1] - 2
    rows = grad_pad.shape[2] - 2
    cols = grad_pad.shape[3] - 2
    total = jnp.zeros((grad_pad.shape[0], depth, rows, cols, grad_pad.shape[4]), jnp.float32)
    for depth_off in range(3):
        for row_off in range(3):
            for col_off in range(3):
                window = grad_pad[
                    :,
                    2 - depth_off : 2 - depth_off + depth,
                    2 - row_off : 2 - row_off + rows,
                    2 - col_off : 2 - col_off + cols,
                ]
                total = total + kernel[depth_off, row_off, col_off] * window.astype(jnp.float32)
    return total


def kernel_terms(padded, grads):
    depth = grads.shape[1]
    rows = grads.shape[2]
    cols = grads.shape[3]
    grads_wide = grads.astype(jnp.float32)
    terms = []
    for depth_off in range(3):
        for row_off in range(3):
            for col_off in range(3):
                window = padded[
                    :,
                    depth_off : depth_off + depth,
                    row_off : row_off + rows,
                    col_off : col_off + cols,
                ]
                terms.append(jnp.sum(window.astype(jnp.float32) * grads_wide, axis=(0, 1, 2, 3)))
    return jnp.stack(terms).reshape(3, 3, 3, grads.shape[4])


def plane_pad(values):
    return jnp.pad(values, ((0, 0), (0, 0), (1, 1), (1, 1), (0, 0)))


def as_sequence(values):
    return values.reshape(1, values.shape[0], -1, values.shape[-1])


def local(
    tokens,
    out_grad,
    first_gain,
    depth_qkv,
    depth_out,
    time_qkv,
    time_out,
    second_gain,
    up_weight,
    spatial_kernel,
    down_weight,
    depth_scale,
    time_scale,
):
    frames, slabs, cells, width = tokens.shape
    base = tokens.astype(jnp.float32)
    norm_first = rounded(normalize(base, first_gain))
    depth_inputs = lax.all_to_all(norm_first, "dev", split_axis=2, concat_axis=1, tiled=True)
    time_inputs = lax.all_to_all(norm_first, "ta", split_axis=2, concat_axis=0, tiled=True)
    all_frames = time_inputs.shape[0]
    depth_fields = rounded(project(depth_inputs, depth_qkv))
    depth_wide, depth_back = jax.vjp(attend, depth_fields.astype(jnp.float32), depth_scale)
    depth_regroup = rounded(depth_wide)
    time_fields = rounded(project(time_inputs, time_qkv))
    time_wide, time_back = jax.vjp(attend, as_sequence(time_fields).astype(jnp.float32), time_scale)
    time_regroup = rounded(time_wide).reshape(all_frames, slabs, -1, width)
    depth_branch = lax.all_to_all(
        rounded(project(depth_regroup, depth_out)), "dev", split_axis=1, concat_axis=2, tiled=True
    )
    time_branch = lax.all_to_all(
        rounded(project(time_regroup, time_out)), "ta", split_axis=0, concat_axis=2, tiled=True
    )
    middle = rounded(base + depth_branch.astype(jnp.float32) + time_branch.astype(jnp.float32))
    middle_wide = middle.astype(jnp.float32)
    norm_second = rounded(normalize(middle_wide, second_gain))
    hidden = rounded(project(norm_second, up_weight))
    shaped = hidden.reshape(frames, slabs, PH, PW, -1)
    rimmed = extended(shaped, (("dev", 1),), 1)
    padded = plane_pad(rimmed)
    filtered = filter_forward(padded, spatial_kernel)
    activated, act_back = jax.vjp(activate, filtered)
    active = rounded(activated).reshape(frames, slabs, cells, -1)
    active_grad = back_project(out_grad, down_weight)
    filtered_grad = rounded(act_back(active_grad.reshape(filtered.shape))[0])
    grad_rim = extended(filtered_grad, (("dev", 1),), 1)
    grad_pad = plane_pad(grad_rim)
    block_out = rounded(middle_wide + project(active, down_weight))
    down_grad = weight_grad(active, out_grad)
    hidden_grad = rounded(filter_backward(grad_pad, spatial_kernel)).reshape(
        frames, slabs, cells, -1
    )
    kernel_grad = kernel_terms(padded, filtered_grad)
    up_grad = weight_grad(norm_second, hidden_grad)
    second_back = back_project(hidden_grad, up_weight)
    norm_out, norm_back = jax.vjp(normalize, middle_wide, second_gain)
    middle_part, second_gain_grad = norm_back(second_back)
    middle_grad = out_grad.astype(jnp.float32) + middle_part
    branch_grad = rounded(middle_grad)
    depth_branch_grad = lax.all_to_all(branch_grad, "dev", split_axis=2, concat_axis=1, tiled=True)
    time_branch_grad = lax.all_to_all(branch_grad, "ta", split_axis=2, concat_axis=0, tiled=True)
    depth_out_grad = weight_grad(depth_regroup, depth_branch_grad)
    time_out_grad = weight_grad(time_regroup, time_branch_grad)
    depth_heads_grad = rounded(back_project(depth_branch_grad, depth_out))
    time_heads_grad = rounded(back_project(time_branch_grad, time_out))
    depth_fields_wide, depth_scale_grad = depth_back(depth_heads_grad.astype(jnp.float32))
    time_fields_wide, time_scale_grad = time_back(as_sequence(time_heads_grad).astype(jnp.float32))
    depth_fields_grad = rounded(depth_fields_wide)
    time_fields_grad = rounded(time_fields_wide).reshape(all_frames, slabs, -1, 3 * width)
    depth_qkv_grad = weight_grad(depth_inputs, depth_fields_grad)
    time_qkv_grad = weight_grad(time_inputs, time_fields_grad)
    depth_first = lax.all_to_all(
        rounded(back_project(depth_fields_grad, depth_qkv)),
        "dev",
        split_axis=1,
        concat_axis=2,
        tiled=True,
    )
    time_first = lax.all_to_all(
        rounded(back_project(time_fields_grad, time_qkv)),
        "ta",
        split_axis=0,
        concat_axis=2,
        tiled=True,
    )
    first_back = depth_first.astype(jnp.float32) + time_first.astype(jnp.float32)
    first_out, first_norm_back = jax.vjp(normalize, base, first_gain)
    base_grad, first_gain_grad = first_norm_back(first_back)
    input_grad = (middle_grad + base_grad).astype(jnp.bfloat16)
    (
        depth_qkv_grad,
        depth_out_grad,
        time_qkv_grad,
        time_out_grad,
        up_grad,
        kernel_grad,
        down_grad,
        first_gain_grad,
        second_gain_grad,
        depth_scale_grad,
        time_scale_grad,
    ) = lax.psum(
        (
            depth_qkv_grad,
            depth_out_grad,
            time_qkv_grad,
            time_out_grad,
            up_grad,
            kernel_grad,
            down_grad,
            first_gain_grad,
            second_gain_grad,
            depth_scale_grad,
            time_scale_grad,
        ),
        ("dev", "ta"),
    )
    factor = 1.0 / math.sqrt(frames * slabs * cells * lax.axis_size("dev") * lax.axis_size("ta"))
    return (
        block_out,
        input_grad,
        depth_qkv_grad * factor,
        depth_out_grad * factor,
        time_qkv_grad * factor,
        time_out_grad * factor,
        up_grad * factor,
        kernel_grad * factor,
        down_grad * factor,
        first_gain_grad * factor,
        second_gain_grad * factor,
        depth_scale_grad * factor,
        time_scale_grad * factor,
    )


def solution(mesh):
    return jax.shard_map(
        local,
        mesh=mesh,
        in_specs=(
            P("ta", "dev", None, None),
            P("ta", "dev", None, None),
            P(),
            P(),
            P(),
            P(),
            P(),
            P(),
            P(),
            P(),
            P(),
            P(),
            P(),
        ),
        out_specs=(
            P("ta", "dev", None, None),
            P("ta", "dev", None, None),
            P(),
            P(),
            P(),
            P(),
            P(),
            P(),
            P(),
            P(),
            P(),
            P(),
            P(),
        ),
        check_vma=False,
    )
```

profile of v0, /device:TPU:0, one launch (start us, length us, event | category | flops | bytes accessed | tf_op | source)
XLA Modules:
  0.0 479.5 jit_solution(5090181505989255509)
XLA Ops:
  12.2 11.7 %all_to_all.102 = bf16[1,2,144,384]{3,1,0,2:T(2,128)(2,1)S(1)} all-to-all(bf16[1,2,144,384]{3,1,0,2:T(2,128)(2,1)} %copy.299), channel_id=1, replica_groups=mesh['dev'=8,'ta'=4] {'dev'}, dimensions={2} | all-to-all | bytes 442368 | tf_op jit(solution)/shard_map/all_to_all | solution.py:158
  23.9 4.9 %all-to-all-start.2 = ((bf16[1,2,144,384]{3,1,0,2:T(2,128)(2,1)}), bf16[1,2,144,384]{3,1,0,2:T(2,128)(2,1)}, u32[]{:S(2)}, u32[]{:S(2)}) async-start(bf16[1,2,144,384]{3,1,0,2:T(2,128)(2,1)} %copy.299), calls=%async_computation.2 | async-start | bytes 442368 | tf_op jit(solution)/shard_map/all_to_all | solution.py:159
  34.2 2.6 reshape.873
  54.8 4.3 all-to-all-start.1
  71.6 4.7 fusion.176
  81.3 5.1 %all-to-all-start.3 = ((bf16[4,2,36,384]{3,1,2,0:T(2,128)(2,1)}), bf16[4,2,36,384]{3,1,2,0:T(2,128)(2,1)S(1)}, u32[]{:S(2)}, u32[]{:S(2)}) async-start(bf16[4,2,36,384]{3,1,2,0:T(2,128)(2,1)} %copy.334), calls=%async_computation.3 | async-start | bytes 442368 | tf_op jit(solution)/shard_map/all_to_all | solution.py:170
  89.7 5.2 %all-to-all-done.3 = bf16[4,2,36,384]{3,1,2,0:T(2,128)(2,1)S(1)} async-done(((bf16[4,2,36,384]{3,1,2,0:T(2,128)(2,1)}), bf16[4,2,36,384]{3,1,2,0:T(2,128)(2,1)S(1)}, u32[]{:S(2)}, u32[]{:S(2)}) %all-to-all-start.3) | async-done | bytes 221216 | tf_op jit(solution)/shard_map/all_to_all | solution.py:170
  101.1 2.9 collective-permute-done.1
  105.3 7.9 %multiply_convert_fusion = (bf16[1,2,6,24,1536]{4,3,2,1,0:T(8,128)(2,1)}, f32[1,2,6,24,1536]{4,3,2,1,0:T(8,128)S(1)}) fusion(bf16[1,4,8,26,1536]{4,3,2,1,0:T(8,128)(2,1)S(1)} %select_maximum_fusion.2, f32[1536]{0:T(1024)S(1)} %get-tuple-element.72, f32[1536]{0:T(1024)S(1)} %get-tuple-element.73, f32[1536]{0:T(1024)S(1)} %get-tuple-element.48, ...), kind=kLoop, calls=%fused_computation.155 | loop fusion | flops 40255488 | bytes 25823232 | tf_op jit(solution)/shard_map/convert_element_type | solution.py:26
  115.0 4.8 %fusion.78 = (f32[1536]{0:T(1024)S(1)}, f32[1536]{0:T(1024)S(1)}, f32[1536]{0:T(1024)S(1)}, f32[1536]{0:T(1024)S(1)}, f32[1536]{0:T(1024)S(1)}, /*index=5*/f32[1...) fusion(bf16[1,2,6,24,1536]{4,3,2,1,0:T(8,128)(2,1)S(1)} %fusion, ...), kind=kLoop, calls=%fused_computation.154 | loop fusion | flops 24302592 | bytes 16920576 | tf_op jit(solution)/shard_map/reduce_sum | solution.py:128
  120.8 10.6 %collective-permute-start.2 = (bf16[1,1,6,24,1536]{4,3,2,1,0:T(8,128)(2,1)}, bf16[1,1,6,24,1536]{4,3,2,1,0:T(8,128)(2,1)}, u32[]{:S(2)}, u32[]{:S(2)}) collective-permute-start(bf16[1,1,6,24,1536]{4,3,2,1,0:T(8,128)(2,1)} %get-tuple-element.93), channel_id=1, source_target_pairs={{0,4},{4,8},{8,12},{12,16},{16,20},{20,24},{24,28},{1,5},{5,9},{9,... | collective-permute-start | bytes 1327112 | tf_op jit(solution)/shard_map/ppermute | solution.py:17
  151.1 5.8 %stack.111 = f32[27,1536]{1,0:T(8,128)} concatenate(f32[1,1536]{1,0:T(1,128)} %stack.84, f32[1,1536]{1,0:T(1,128)} %stack.85, f32[1,1536]{1,0:T(1,128)} %stack.86, f32[1,1536]{1,0:T(1,128)} %stack.87, f32[1,1536]{1,0:T(1,128)} %stack.88, f32[1,1536]{1,0:T(1,128)} %stack.89, f32[1,1536]{1,0:T(1,128)} %stack.90, f32[1,1536]{1,0:T(1,128)} %stack.91, f32[1,1536]{1,0:T(1,128)} %stack.92, ...), dimensions={0} | concatenate | bytes 331776 | tf_op jit(solution)/shard_map/stack | solution.py:129
  158.6 3.5 convolution_bitcast_fusion.1
  164.8 7.6 %fusion.79 = bf16[1,2,6,24,1536]{4,3,2,1,0:T(8,128)(2,1)S(1)} fusion(bf16[1,2,6,24,1536]{4,3,2,1,0:T(8,128)(2,1)S(1)} %fusion.35, bf16[1,4,8,26,1536]{4,3,2,1,0:T(8,128)(2,1)S(1)} %select_maximum_fusion, bf16[1,1,6,24,1536]{4,3,2,1,0:T(8,128)(2,1)} %collective-permute-done.2, bf16[1,1,6,24,1536]{4,3,2,1,0:T(8,128)(2,1)} %collective-permute-done.3, ...), kind=kLoop, calls=%fused_computation.156 | loop fusion | flops 36716544 | bytes 24053760 | tf_op jit(solution)/shard_map/convert_element_type | solution.py:26
  175.2 4.0 all-to-all-start.4
  181.5 4.3 all-to-all-done.4
  185.8 4.0 all-to-all-start.6
  194.8 3.5 multiply_reduce_fusion.5
  198.3 3.0 multiply_reduce_fusion.6
  228.6 4.2 convolution_bitcast_fusion.7
  235.2 4.6 fusion.102
  239.8 4.0 fusion.104
  255.1 3.1 convolution_bitcast_fusion.3
  259.3 2.7 fusion.91
  262.0 3.4 all-to-all-start.5
  268.0 8.1 %all-to-all-done.5 = bf16[1,16,18,384]{3,2,0,1:T(8,128)(2,1)S(1)} async-done(((bf16[1,16,18,384]{3,2,0,1:T(8,128)(2,1)}), bf16[1,16,18,384]{3,2,0,1:T(8,128)(2,1)S(1)}, u32[]{:S(2)}, u32[]{:S(2)}) %all-to-all-start.5) | async-done | bytes 221216 | tf_op jit(solution)/shard_map/all_to_all | solution.py:211
  276.1 5.0 %all-to-all-start.7 = ((bf16[4,2,36,384]{3,1,2,0:T(2,128)(2,1)}), bf16[4,2,36,384]{3,1,2,0:T(2,128)(2,1)S(1)}, u32[]{:S(2)}, u32[]{:S(2)}) async-start(bf16[4,2,36,384]{3,1,2,0:T(2,128)(2,1)} %copy.379), calls=%async_computation.7 | async-start | bytes 442368 | tf_op jit(solution)/shard_map/all_to_all | solution.py:218
  281.1 2.9 fusion.83
  284.7 6.0 %all-to-all-done.7 = bf16[4,2,36,384]{3,1,2,0:T(2,128)(2,1)S(1)} async-done(((bf16[4,2,36,384]{3,1,2,0:T(2,128)(2,1)}), bf16[4,2,36,384]{3,1,2,0:T(2,128)(2,1)S(1)}, u32[]{:S(2)}, u32[]{:S(2)}) %all-to-all-start.7) | async-done | bytes 221216 | tf_op jit(solution)/shard_map/all_to_all | solution.py:218
  291.6 40.8 %all-reduce.8 = (f32[384]{0:T(512)S(1)}, f32[384]{0:T(512)S(1)}, f32[6]{0:T(128)S(1)}, f32[6]{0:T(128)S(1)}) all-reduce(f32[384]{0:T(512)S(1)} %get-tuple-element.45, f32[384]{0:T(512)S(1)} %copy-done.160, f32[6]{0:T(128)S(1)} %multiply_reduce_fusion.3, f32[6]{0:T(128)S(1)} %get-tuple-element.85), channel_id=1, replica_groups=mesh['dev'=8,'ta'=4] {'dev','ta'}, use_global_device_ids=true, to_apply=%region_55.56 | all-reduce | flops 780 | bytes 6240 | tf_op jit(solution)/shard_map/psum | solution.py:241
  335.7 124.6 %all-reduce.12.cloned.1.call-done = (f32[384,1152]{1,0:T(8,128)}, f32[384,384]{1,0:T(8,128)}, f32[384,1152]{1,0:T(8,128)}, f32[384,384]{1,0:T(8,128)}, f32[384,1...) async-done(((f32[384,1152]{1,0:T(8,128)}, f32[384,384]{1,0:T(8,128)}, f32[384,1152]{1,0:T(8,128)}, f32[384,384]{1,0:T(8,128)}, f32[384,1536]{1,0:T(8,128)}, ...) | async-done | bytes 9603088 | tf_op jit(solution)/shard_map/psum | solution.py:241
  460.3 2.9 broadcast_multiply_fusion.3
  (511 shorter events, 149.9 us)
Async XLA Ops:
  7.2 88.7 %copy-start = (bf16[384,1536]{1,0:T(8,128)(2,1)S(1)}, bf16[384,1536]{1,0:T(8,128)(2,1)}, u32[]{:S(2)}) copy-start(bf16[384,1536]{1,0:T(8,128)(2,1)} %param.21) | copy-start | bytes 3538948
  7.2 21.6 %copy-start.56 = (bf16[384,1152]{1,0:T(8,128)(2,1)S(1)}, bf16[384,1152]{1,0:T(8,128)(2,1)}, u32[]{:S(2)}) copy-start(bf16[384,1152]{1,0:T(8,128)(2,1)} %param.16) | copy-start | bytes 2654212
  23.9 30.9 %all-to-all-start.2 = ((bf16[1,2,144,384]{3,1,0,2:T(2,128)(2,1)}), bf16[1,2,144,384]{3,1,0,2:T(2,128)(2,1)}, u32[]{:S(2)}, u32[]{:S(2)}) async-start(bf16[1,2,144,384]{3,1,0,2:T(2,128)(2,1)} %copy.299), calls=%async_computation.2 | async-start | bytes 442368 | tf_op jit(solution)/shard_map/all_to_all | solution.py:159
  54.8 26.5 %all-to-all-start.1 = ((bf16[1,16,18,384]{3,2,0,1:T(8,128)(2,1)}), bf16[1,16,18,384]{3,2,0,1:T(8,128)(2,1)}, u32[]{:S(2)}, u32[]{:S(2)}) async-start(bf16[1,16,18,384]{3,2,0,1:T(8,128)(2,1)} %bitcast.10), calls=%async_computation.1 | async-start | bytes 589824 | tf_op jit(solution)/shard_map/all_to_all | solution.py:167
  81.3 13.7 %all-to-all-start.3 = ((bf16[4,2,36,384]{3,1,2,0:T(2,128)(2,1)}), bf16[4,2,36,384]{3,1,2,0:T(2,128)(2,1)S(1)}, u32[]{:S(2)}, u32[]{:S(2)}) async-start(bf16[4,2,36,384]{3,1,2,0:T(2,128)(2,1)} %copy.334), calls=%async_computation.3 | async-start | bytes 442368 | tf_op jit(solution)/shard_map/all_to_all | solution.py:170
  86.5 18.5 %copy-start.94 = (f32[1536]{0:T(1024)}, f32[1536]{0:T(1024)S(1)}, u32[]{:S(2)}) copy-start(f32[1536]{0:T(1024)S(1)} %get-tuple-element.68) | copy-start | bytes 18436
  86.5 18.5 %copy-start.96 = (f32[1536]{0:T(1024)}, f32[1536]{0:T(1024)S(1)}, u32[]{:S(2)}) copy-start(f32[1536]{0:T(1024)S(1)} %get-tuple-element.69) | copy-start | bytes 18436
  86.5 18.5 %copy-start.98 = (f32[1536]{0:T(1024)}, f32[1536]{0:T(1024)S(1)}, u32[]{:S(2)}) copy-start(f32[1536]{0:T(1024)S(1)} %get-tuple-element.70) | copy-start | bytes 18436
  86.5 18.5 %copy-start.100 = (f32[1536]{0:T(1024)}, f32[1536]{0:T(1024)S(1)}, u32[]{:S(2)}) copy-start(f32[1536]{0:T(1024)S(1)} %get-tuple-element.71) | copy-start | bytes 18436
  86.5 18.5 %copy-start.102 = (f32[1536]{0:T(1024)}, f32[1536]{0:T(1024)S(1)}, u32[]{:S(2)}) copy-start(f32[1536]{0:T(1024)S(1)} %get-tuple-element.72) | copy-start | bytes 18436
  86.6 18.5 %copy-start.104 = (f32[1536]{0:T(1024)}, f32[1536]{0:T(1024)S(1)}, u32[]{:S(2)}) copy-start(f32[1536]{0:T(1024)S(1)} %get-tuple-element.73) | copy-start | bytes 18436
  86.9 18.2 %copy-start.106 = (f32[1536]{0:T(1024)}, f32[1536]{0:T(1024)S(1)}, u32[]{:S(2)}) copy-start(f32[1536]{0:T(1024)S(1)} %get-tuple-element.47) | copy-start | bytes 18436
  86.9 18.2 %copy-start.108 = (f32[1536]{0:T(1024)}, f32[1536]{0:T(1024)S(1)}, u32[]{:S(2)}) copy-start(f32[1536]{0:T(1024)S(1)} %get-tuple-element.48) | copy-start | bytes 18436
  86.9 18.2 %copy-start.110 = (f32[1536]{0:T(1024)}, f32[1536]{0:T(1024)S(1)}, u32[]{:S(2)}) copy-start(f32[1536]{0:T(1024)S(1)} %get-tuple-element.49) | copy-start | bytes 18436
  95.4 78.7 %copy-start.90 = (f32[2,144]{1,0:T(2,128)}, f32[2,144]{1,0:T(2,128)S(1)}, u32[]{:S(2)}) copy-start(f32[2,144]{1,0:T(2,128)S(1)} %broadcast_multiply_fusion.13) | copy-start | bytes 3460
  95.7 78.4 %copy-start.92 = (f32[2,144]{1,0:T(2,128)}, f32[2,144]{1,0:T(2,128)S(1)}, u32[]{:S(2)}) copy-start(f32[2,144]{1,0:T(2,128)S(1)} %fusion.173) | copy-start | bytes 3460
  96.6 4.5 collective-permute-start
  98.4 5.6 %collective-permute-start.1 = (bf16[1,1,6,24,1536]{4,3,2,1,0:T(8,128)(2,1)S(1)}, bf16[1,1,6,24,1536]{4,3,2,1,0:T(8,128)(2,1)S(1)}, u32[]{:S(2)}, u32[]{:S(2)}) collective-permute-start(bf16[1,1,6,24,1536]{4,3,2,1,0:T(8,128)(2,1)S(1)} %get-tuple-element.96), channel_id=1, source_target_pairs={{4,0},{8,4},{12,8},{16,12},{20,16},{24,20},{28,24},{5,1},{9,5},{13... | collective-permute-start | bytes 1327112 | tf_op jit(solution)/shard_map/ppermute | solution.py:20
  120.8 41.5 %collective-permute-start.2 = (bf16[1,1,6,24,1536]{4,3,2,1,0:T(8,128)(2,1)}, bf16[1,1,6,24,1536]{4,3,2,1,0:T(8,128)(2,1)}, u32[]{:S(2)}, u32[]{:S(2)}) collective-permute-start(bf16[1,1,6,24,1536]{4,3,2,1,0:T(8,128)(2,1)} %get-tuple-element.93), channel_id=1, source_target_pairs={{0,4},{4,8},{8,12},{12,16},{16,20},{20,24},{24,28},{1,5},{5,9},{9,... | collective-permute-start | bytes 1327112 | tf_op jit(solution)/shard_map/ppermute | solution.py:17
  131.4 31.0 %collective-permute-start.3 = (bf16[1,1,6,24,1536]{4,3,2,1,0:T(8,128)(2,1)}, bf16[1,1,6,24,1536]{4,3,2,1,0:T(8,128)(2,1)}, u32[]{:S(2)}, u32[]{:S(2)}) collective-permute-start(bf16[1,1,6,24,1536]{4,3,2,1,0:T(8,128)(2,1)} %get-tuple-element.94), channel_id=1, source_target_pairs={{4,0},{8,4},{12,8},{16,12},{20,16},{24,20},{28,24},{5,1},{9,5},{13... | collective-permute-start | bytes 1327112 | tf_op jit(solution)/shard_map/ppermute | solution.py:20
  175.2 10.5 %all-to-all-start.4 = ((bf16[1,2,144,384]{3,1,0,2:T(2,128)(2,1)}), bf16[1,2,144,384]{3,1,0,2:T(2,128)(2,1)}, u32[]{:S(2)}, u32[]{:S(2)}) async-start(bf16[1,2,144,384]{3,1,0,2:T(2,128)(2,1)} %copy.336), calls=%async_computation.4 | async-start | bytes 442368 | tf_op jit(solution)/shard_map/all_to_all | solution.py:199
  185.8 38.1 %all-to-all-start.6 = ((bf16[1,2,144,384]{3,1,0,2:T(2,128)(2,1)}), bf16[1,2,144,384]{3,1,0,2:T(2,128)(2,1)}, u32[]{:S(2)}, u32[]{:S(2)}) async-start(bf16[1,2,144,384]{3,1,0,2:T(2,128)(2,1)} %copy.336), calls=%async_computation.6 | async-start | bytes 442368 | tf_op jit(solution)/shard_map/all_to_all | solution.py:200
  189.8 270.5 %all-reduce.12.cloned.1.call-start = ((), (), s32[]{:S(2)}) async-start(), calls=%async_computation.8 | async-start | bytes 19316736 | tf_op jit(solution)/shard_map/psum | solution.py:241
  262.0 14.1 %all-to-all-start.5 = ((bf16[1,16,18,384]{3,2,0,1:T(8,128)(2,1)}), bf16[1,16,18,384]{3,2,0,1:T(8,128)(2,1)S(1)}, u32[]{:S(2)}, u32[]{:S(2)}) async-start(bf16[1,16,18,384]{3,2,0,1:T(8,128)(2,1)} %bitcast.65), calls=%async_computation.5 | async-start | bytes 589824 | tf_op jit(solution)/shard_map/all_to_all | solution.py:211
  276.1 14.6 %all-to-all-start.7 = ((bf16[4,2,36,384]{3,1,2,0:T(2,128)(2,1)}), bf16[4,2,36,384]{3,1,2,0:T(2,128)(2,1)S(1)}, u32[]{:S(2)}, u32[]{:S(2)}) async-start(bf16[4,2,36,384]{3,1,2,0:T(2,128)(2,1)} %copy.379), calls=%async_computation.7 | async-start | bytes 442368 | tf_op jit(solution)/shard_map/all_to_all | solution.py:218
  284.5 50.2 %copy-start.18 = (f32[2,144,384]{2,1,0:T(8,128)S(1)}, f32[2,144,384]{2,1,0:T(8,128)}, u32[]{:S(2)}) copy-start(f32[2,144,384]{2,1,0:T(8,128)} %copy-done.17) | copy-start | bytes 1327108
  284.5 50.2 %copy-start.37 = (bf16[1,2,144,384]{3,2,1,0:T(8,128)(2,1)S(1)}, bf16[1,2,144,384]{3,2,1,0:T(8,128)(2,1)}, u32[]{:S(2)}) copy-start(bf16[1,2,144,384]{3,2,1,0:T(8,128)(2,1)} %param.14) | copy-start | bytes 663556
  284.5 50.1 %copy-start.91 = (f32[2,144]{1,0:T(2,128)S(1)}, f32[2,144]{1,0:T(2,128)}, u32[]{:S(2)}) copy-start(f32[2,144]{1,0:T(2,128)} %copy-done.90) | copy-start | bytes 3460
  284.5 50.1 %copy-start.93 = (f32[2,144]{1,0:T(2,128)S(1)}, f32[2,144]{1,0:T(2,128)}, u32[]{:S(2)}) copy-start(f32[2,144]{1,0:T(2,128)} %copy-done.92) | copy-start | bytes 3460
  284.5 50.1 %copy-start.147 = (f32[384]{0:T(512)S(1)}, f32[384]{0:T(512)}, u32[]{:S(2)}) copy-start(f32[384]{0:T(512)} %param.20) | copy-start | bytes 4612
  284.5 50.1 %copy-start.149 = (f32[2,144]{1,0:T(2,128)S(1)}, f32[2,144]{1,0:T(2,128)}, u32[]{:S(2)}) copy-start(f32[2,144]{1,0:T(2,128)} %copy-done.148) | copy-start | bytes 3460
  284.5 50.1 %copy-start.153 = (f32[2,144]{1,0:T(2,128)S(1)}, f32[2,144]{1,0:T(2,128)}, u32[]{:S(2)}) copy-start(f32[2,144]{1,0:T(2,128)} %copy-done.152) | copy-start | bytes 3460
  (145 other events, 823.5 us)
Sparse Core Ops, SparseCore 0:
  258.4 201.9 all-reduce.11
where the time goes:
time: 489 us; the launch traced here: 479 us
  waiting for transfers between devices  151 us (31%)
  local copies, waits for them, and re-layouts  85.5 us (17%)
  other arithmetic  64.3 us (13%)
  matrix products  63.3 us (13%)
  blocking collectives  52.5 us (11%)
  starting transfers between devices  45.9 us (9%)
  between operations  16.9 us (3%)
    psum x1, waiting for transfers between devices, local(): lax.psum((depth_qkv_grad, depth_out_grad, time_qkv_grad, time_out_grad, u...  125 us
    psum x1, blocking collectives, local(): lax.psum((depth_qkv_grad, depth_out_grad, time_qkv_grad, time_out_grad, u...  40.8 us
    another operation x28, local copies, waits for them, and re-layouts, kernel_terms(): return jnp.stack(terms).reshape(3, 3, 3, grads.shape[4])  22 us
    dot_general x6, matrix products, attend(): jnp.einsum('plbhd,pmbhd->pbhlm', query, keyed, precision=lax.Precision.HI...  21.5 us
    convert_element_type x8, other arithmetic, rounded(): return lax.optimization_barrier(values.astype(jnp.bfloat16))  18.7 us
    dot_general x6, matrix products, weight_grad(): lax.dot_general(left, grads, ((lead, lead), ((), ())), preferred_element_...  14.1 us
    ppermute x2, starting transfers between devices, extended(): lax.ppermute(lax.slice_in_dim(block, block.shape[dim] - width, None, axis...  12.4 us
    dot_general x6, matrix products, attend(): jnp.einsum('pbhlm,pmbhd->plbhd', weights, valued, precision=lax.Precision...  11.9 us
  transfers between devices with their start and end apart: 12, of which 6 were waited for; matrix products, arithmetic and copies ran while one was open for 27% of the time, Pallas kernels for 0%

commit v1 on v0

v1 whole, which is shorter than its diff:
```python
import functools
import math

import jax
import jax.numpy as jnp
import numpy as np
from jax import lax
from jax.experimental import pallas as pl
from jax.experimental.pallas import tpu as pltpu
from jax.sharding import PartitionSpec as P

PH = 6
PW = 24
LANES = 128
CHUNK = 256
BF = jnp.bfloat16
F32 = jnp.float32
MESH = pl.DeviceIdType.MESH
VMEM_BYTES = 56 * 1024 * 1024

VM = pl.BlockSpec(memory_space=pltpu.VMEM)
SM = pl.BlockSpec(memory_space=pltpu.SMEM)


def dot(left, right):
    return jnp.dot(left, right, preferred_element_type=F32)


def dot_nt(left, right):
    return lax.dot_general(left, right, (((1,), (1,)), ((), ())), preferred_element_type=F32)


def dot_tn(left, right):
    return lax.dot_general(left, right, (((0,), (0,)), ((), ())), preferred_element_type=F32)


def params(**more):
    return pltpu.CompilerParams(vmem_limit_bytes=VMEM_BYTES, **more)


def standard(values):
    centered = values - jnp.mean(values, axis=-1, keepdims=True)
    spread = jnp.mean(centered * centered, axis=-1, keepdims=True)
    inverse = lax.rsqrt(spread + 1e-05)
    return centered * inverse, inverse


def norm_back(values, gain, back):
    high, inverse = standard(values)
    inner = back * gain
    part = inner - jnp.mean(inner, axis=-1, keepdims=True)
    part = part - high * jnp.mean(inner * high, axis=-1, keepdims=True)
    return part * inverse, jnp.sum(back * high, axis=0, keepdims=True)


def exchange_kernel(nd, nt, sd, st, rd, rt, send_d, recv_d, send_t, recv_t):
    d = lax.axis_index("dev")
    t = lax.axis_index("ta")
    barrier = pltpu.get_barrier_semaphore()
    for off in range(1, nd):
        peer = lax.rem(d + off, nd)
        pl.semaphore_signal(barrier, inc=1, device_id=(peer, t), device_id_type=MESH)
    for off in range(1, nt):
        peer = lax.rem(t + off, nt)
        pl.semaphore_signal(barrier, inc=1, device_id=(d, peer), device_id_type=MESH)
    pl.semaphore_wait(barrier, nd + nt - 2)
    copies = []
    for off in range(1, nt):
        peer = lax.rem(t + off, nt)
        copies.append(
            pltpu.make_async_remote_copy(
                src_ref=st.at[peer],
                dst_ref=rt.at[t],
                send_sem=send_t.at[off - 1],
                recv_sem=recv_t.at[off - 1],
                device_id=(d, peer),
                device_id_type=MESH,
            )
        )
    for off in range(1, nd):
        peer = lax.rem(d + off, nd)
        copies.append(
            pltpu.make_async_remote_copy(
                src_ref=sd.at[peer],
                dst_ref=rd.at[d],
                send_sem=send_d.at[off - 1],
                recv_sem=recv_d.at[off - 1],
                device_id=(peer, t),
                device_id_type=MESH,
            )
        )
    for copy in copies:
        copy.start()
    rd[d] = sd[d]
    rt[t] = st[t]
    for copy in copies:
        copy.wait()


def exchange(send_d, send_t, nd, nt):
    width = send_d.shape[-1]
    sd = send_d.reshape(nd, -1, width)
    st = send_t.reshape(nt, -1, width)
    rd, rt = pl.pallas_call(
        functools.partial(exchange_kernel, nd, nt),
        out_shape=(
            jax.ShapeDtypeStruct(sd.shape, sd.dtype),
            jax.ShapeDtypeStruct(st.shape, st.dtype),
        ),
        in_specs=[VM, VM],
        out_specs=(VM, VM),
        scratch_shapes=[
            pltpu.SemaphoreType.DMA((nd - 1,)),
            pltpu.SemaphoreType.DMA((nd - 1,)),
            pltpu.SemaphoreType.DMA((nt - 1,)),
            pltpu.SemaphoreType.DMA((nt - 1,)),
        ],
        compiler_params=pltpu.CompilerParams(
            collective_id=0, has_side_effects=True, vmem_limit_bytes=VMEM_BYTES
        ),
        name="exchange",
    )(sd, st)
    return rd.reshape(send_d.shape), rt.reshape(send_t.shape)


def first_kernel(tokens, gain, pd, pt, out_d, out_t):
    high, _ = standard(tokens[...].astype(F32))
    normed = (high * gain[...]).astype(BF)
    out_d[...] = dot(pd[...], normed).astype(BF)
    out_t[...] = dot(pt[...], normed).astype(BF)


def attend_forward(x, qkv, out, mask, scale, fields, mixed_t, branch, qs, ks, vt):
    rows, width = x.shape
    heads = scale.shape[0]
    size = width // heads
    full = dot(x[...], qkv[...]).astype(BF)
    fields[...] = full
    wide = full.astype(F32)
    qs[...] = wide[:, :width].T
    ks[...] = wide[:, width : 2 * width]
    vt[...] = wide[:, 2 * width :].T.astype(BF)
    for head in range(heads):
        part = slice(head * size, (head + 1) * size)
        query = qs[part, :]
        factor = lax.rsqrt(jnp.sum(query * query, axis=0, keepdims=True) + 1e-06) * scale[head]
        query = query.astype(BF)
        keyed = ks[:, part]
        keyed = keyed * lax.rsqrt(jnp.sum(keyed * keyed, axis=1, keepdims=True) + 1e-06)
        keyed = keyed.astype(BF)
        valued = vt[part, :]
        for start in range(0, rows, LANES):
            cols = slice(start, start + LANES)
            score = dot(keyed, query[:, cols]) * factor[:, cols]
            raised = jnp.exp(score) * mask[:, cols]
            total = jnp.sum(raised, axis=0, keepdims=True)
            mixed = dot(valued, raised.astype(BF)) / total
            mixed_t[part, cols] = mixed.astype(BF)
    mixed = mixed_t[...].astype(F32).T.astype(BF)
    branch[...] = dot(mixed, out[...]).astype(BF)


def attention_kernel(
    scale_d, scale_t, xd, xt, qkv_d, out_d, qkv_t, out_t, mask_d, mask_t,
    fields_d, mixed_d, branch_d, fields_t, mixed_t, branch_t, qs, ks, vt, qs2, ks2, vt2,
):
    attend_forward(xd, qkv_d, out_d, mask_d, scale_d, fields_d, mixed_d, branch_d, qs, ks, vt)
    attend_forward(xt, qkv_t, out_t, mask_t, scale_t, fields_t, mixed_t, branch_t, qs2, ks2, vt2)


def attend_backward(
    x, grads, fields, mixed_t, qkv, out, mask, scale, factor,
    first, qkv_grad, out_grad, scale_grad, qt, kt, gt, natural, dqt, dfields,
):
    rows, width = x.shape
    heads = scale.shape[0]
    size = width // heads
    cot = grads[...]
    out_grad[...] = (dot(mixed_t[...], cot) * factor).astype(BF)
    heads_grad = dot_nt(cot, out[...]).astype(BF)
    gt[...] = heads_grad.astype(F32).T.astype(BF)
    wide = fields[...].astype(F32)
    natural[:, :width] = wide[:, : width]
    natural[:, width : 2 * width] = wide[:, width : 2 * width]
    natural[:, 2 * width :] = heads_grad.astype(F32)
    qt[...] = wide[:, :width].T
    kt[...] = wide[:, width : 2 * width].T
    for head in range(heads):
        lo, hi = head * size, (head + 1) * size
        part = slice(lo, hi)
        by = scale[head]
        query = qt[part, :]
        inverse_q = lax.rsqrt(jnp.sum(query * query, axis=0, keepdims=True) + 1e-06)
        query_t = query * inverse_q
        query = query.astype(BF)
        query_n = natural[:, lo:hi]
        query_n = query_n * lax.rsqrt(jnp.sum(query_n * query_n, axis=1, keepdims=True) + 1e-06)
        query_n = query_n.astype(BF)
        keyed = natural[:, width + lo : width + hi]
        inverse_k = lax.rsqrt(jnp.sum(keyed * keyed, axis=1, keepdims=True) + 1e-06)
        keyed = keyed * inverse_k
        keyed_b = keyed.astype(BF)
        key_t = kt[part, :]
        key_t = key_t * lax.rsqrt(jnp.sum(key_t * key_t, axis=0, keepdims=True) + 1e-06)
        key_t = key_t.astype(BF)
        valued = fields[:, 2 * width + lo : 2 * width + hi]
        weights, slopes = [], []
        for start in range(0, rows, LANES):
            cols = slice(start, start + LANES)
            inverse = inverse_q[:, cols]
            cosine = dot(keyed_b, query[:, cols]) * inverse
            raised = jnp.exp(cosine * by) * mask[:, cols]
            weight = raised * (1.0 / jnp.sum(raised, axis=0, keepdims=True))
            slope = dot(valued, gt[part, cols])
            delta = jnp.sum(weight * slope, axis=0, keepdims=True)
            slope = weight * (slope - delta)
            scale_grad[head : head + 1, cols] = jnp.sum(slope * cosine, axis=0, keepdims=True)
            slope = (slope * by).astype(BF)
            weights.append(weight.astype(BF))
            slopes.append(slope)
            back = dot(key_t, slope)
            unit = query_t[:, cols]
            back = back - unit * jnp.sum(back * unit, axis=0, keepdims=True)
            dqt[part, cols] = back * inverse
        weight = jnp.concatenate(weights, axis=1)
        slope = jnp.concatenate(slopes, axis=1)
        dfields[:, 2 * width + lo : 2 * width + hi] = dot(
            weight, natural[:, 2 * width + lo : 2 * width + hi].astype(BF)
        )
        back = dot(slope, query_n)
        back = back - keyed * jnp.sum(back * keyed, axis=1, keepdims=True)
        dfields[:, width + lo : width + hi] = back * inverse_k
    dfields[:, :width] = dqt[...].T
    narrow = dfields[...].astype(BF)
    first[...] = dot_nt(narrow, qkv[...]).astype(BF)
    turned = x[...].astype(F32).T.astype(BF)
    qkv_grad[...] = (dot(turned, narrow) * factor).astype(BF)


def attention_back_kernel(
    factor, scale_d, scale_t, xd, xt, gd, gt_, fields_d, fields_t, mixed_d, mixed_t,
    qkv_d, out_d, qkv_t, out_t, mask_d, mask_t,
    first_d, first_t, qkv_grad_d, qkv_grad_t, out_grad_d, out_grad_t, sg_d, sg_t, *scratch,
):
    attend_backward(
        xd, gd, fields_d, mixed_d, qkv_d, out_d, mask_d, scale_d, factor,
        first_d, qkv_grad_d, out_grad_d, sg_d, *scratch[:6],
    )
    attend_backward(
        xt, gt_, fields_t, mixed_t, qkv_t, out_t, mask_t, scale_t, factor,
        first_t, qkv_grad_t, out_grad_t, sg_t, *scratch[6:],
    )


def middle_kernel(tokens, bd, bt, pdt, ptt, middle):
    depth_part = dot(pdt[...], bd[...])
    time_part = dot(ptt[...], bt[...])
    middle[...] = (tokens[...].astype(F32) + depth_part + time_part).astype(BF)


def shifted(values):
    rows = values.shape[0]
    column = lax.broadcasted_iota(jnp.int32, values.shape, 0) % PW
    left = jnp.where(column == 0, 0.0, pltpu.roll(values, 1, 0))
    right = jnp.where(column == PW - 1, 0.0, pltpu.roll(values, rows - 1, 0))
    return (left, values, right)


def fill_windows(windows, slab, values):
    cells = values.shape[0]
    for off, moved in enumerate(shifted(values)):
        windows[off, slab, PW : PW + cells, :] = moved


def clear_rims(windows, cells):
    slabs = windows.shape[1]
    blank = jnp.zeros((PW, windows.shape[3]), F32)
    for off in range(3):
        for slab in range(slabs):
            windows[off, slab, 0:PW, :] = blank
            windows[off, slab, PW + cells : 2 * PW + cells, :] = blank


def feed_kernel(
    factor, slabs, cells, low, mid, high, gain, og, up, kernel, down,
    fg, block_out, down_grad, kernel_grad, normed_out, normed, windows, total, active,
):
    step = pl.program_id(0)
    own = slabs * cells

    @pl.when(step == 0)
    def _():
        for start, source in ((0, low), (cells, mid), (cells + own, high)):
            values = source[...].astype(F32)
            unit, _ = standard(values)
            normed[start : start + values.shape[0], :] = (unit * gain[...]).astype(BF)
        normed_out[...] = normed[cells : cells + own, :]
        total[...] = mid[...].astype(F32)
        clear_rims(windows, cells)

    for slab in range(slabs + 2):
        hidden = dot(normed[slab * cells : (slab + 1) * cells, :], up[...])
        fill_windows(windows, slab, hidden.astype(BF).astype(F32))
    for slab in range(slabs):
        rows = slice(slab * cells, (slab + 1) * cells)
        slope = dot_nt(og[rows, :], down[...])
        for start in range(0, CHUNK, LANES):
            lanes = slice(start, start + LANES)
            value = jnp.zeros((cells, LANES), F32)
            for a in range(3):
                for b in range(3):
                    for e in range(3):
                        tap = a * 9 + b * 3 + e
                        window = windows[e, slab + a, b * PW : b * PW + cells, lanes]
                        value = value + kernel[tap : tap + 1, lanes] * window
            square = value * value
            bent = jnp.tanh(0.7978845608 * value * (1.0 + 0.044715 * square))
            half = 0.5 * (1.0 + bent)
            active[rows, lanes] = (value * half).astype(BF)
            tilt = half + 0.5 * value * (1.0 - bent * bent) * (
                0.7978845608 * (1.0 + 3.0 * 0.044715 * square)
            )
            fg[rows, lanes] = (slope[:, lanes] * tilt).astype(BF)
    for start in range(0, CHUNK, LANES):
        lanes = slice(start, start + LANES)
        for a in range(3):
            for b in range(3):
                for e in range(3):
                    tap = a * 9 + b * 3 + e
                    sums = jnp.zeros((8, LANES), F32)
                    for slab in range(slabs):
                        window = windows[e, slab + a, b * PW : b * PW + cells, lanes]
                        grads = fg[slab * cells : (slab + 1) * cells, lanes].astype(F32)
                        sums = sums + jnp.sum((window * grads).reshape(cells // 8, 8, LANES), axis=0)
                    kernel_grad[tap : tap + 1, lanes] = factor * jnp.sum(sums, axis=0, keepdims=True)
    total[...] += dot(active[...], down[...])
    down_grad[...] = (factor * dot_tn(active[...], og[...])).astype(BF)

    @pl.when(step == pl.num_programs(0) - 1)
    def _():
        block_out[...] = total[...].astype(BF)


def feed_back_kernel(
    factor, slabs, cells, low, fg, high, kernel, up, normed, mid, og, gain, pd, pt,
    up_grad, middle_grad, send_d, send_t, gain_grad, windows, turned, total, hidden,
):
    step = pl.program_id(0)

    @pl.when(step == 0)
    def _():
        total[...] = jnp.zeros_like(total)
        clear_rims(windows, cells)

    for slab in range(slabs + 2):
        if slab == 0:
            values = low[...]
        elif slab == slabs + 1:
            values = high[...]
        else:
            values = fg[(slab - 1) * cells : slab * cells, :]
        fill_windows(windows, slab, values.astype(F32))
    for slab in range(slabs):
        rows = slice(slab * cells, (slab + 1) * cells)
        for start in range(0, CHUNK, LANES):
            lanes = slice(start, start + LANES)
            value = jnp.zeros((cells, LANES), F32)
            for a in range(3):
                for b in range(3):
                    for e in range(3):
                        tap = (2 - a) * 9 + (2 - b) * 3 + (2 - e)
                        window = windows[e, slab + a, b * PW : b * PW + cells, lanes]
                        value = value + kernel[tap : tap + 1, lanes] * window
            hidden[rows, lanes] = value.astype(BF)
    total[...] += dot_nt(hidden[...], up[...])
    up_grad[...] = (factor * dot_tn(normed[...], hidden[...])).astype(BF)

    @pl.when(step == pl.num_programs(0) - 1)
    def _():
        part, gains = norm_back(mid[...].astype(F32), gain[...], total[...])
        gain_grad[...] = gains
        grads = og[...].astype(F32) + part
        middle_grad[...] = grads
        narrow = grads.astype(BF)
        send_d[...] = dot(pd[...], narrow).astype(BF)
        send_t[...] = dot(pt[...], narrow).astype(BF)


def last_kernel(tokens, gain, fd, ft, pdt, ptt, middle_grad, input_grad, gain_grad):
    back = dot(pdt[...], fd[...]) + dot(ptt[...], ft[...])
    part, gains = norm_back(tokens[...].astype(F32), gain[...], back)
    gain_grad[...] = gains
    input_grad[...] = (middle_grad[...] + part).astype(BF)


def placement(groups, slabs, cells):
    each = cells // groups
    padded = -(-each // 8) * 8
    while (slabs * padded) % 16 or (groups * slabs * padded) % LANES:
        padded += 8
    rows = groups * slabs * padded
    index = np.arange(rows)
    group, slab, cell = index // (slabs * padded), index // padded % slabs, index % padded
    token = slab * cells + group * each + cell
    hot = (token[:, None] == np.arange(slabs * cells)[None, :]) & (cell < each)[:, None]
    return padded, hot.astype(np.float32), cell, slab


def shape(dims, kind):
    return jax.ShapeDtypeStruct(dims, kind)


def local(
    tokens,
    out_grad,
    first_gain,
    depth_qkv,
    depth_out,
    time_qkv,
    time_out,
    second_gain,
    up_weight,
    spatial_kernel,
    down_weight,
    depth_scale,
    time_scale,
):
    frames, slabs, cells, width = tokens.shape
    assert frames == 1 and cells == PH * PW
    nd, nt = lax.axis_size("dev"), lax.axis_size("ta")
    heads = depth_scale.shape[0]
    hid = up_weight.shape[1]
    own = slabs * cells
    factor = 1.0 / math.sqrt(frames * slabs * cells * nd * nt)

    _, hot_d, cell_d, _ = placement(nd, slabs, cells)
    _, hot_t, cell_t, slab_t = placement(nt, slabs, cells)
    rows_d, rows_t = hot_d.shape[0], hot_t.shape[0]
    mask_d = jnp.asarray((cell_d[:, None] == cell_d[None, :]).astype(np.float32))
    same = (cell_t[:, None] == cell_t[None, :]) & (slab_t[:, None] == slab_t[None, :])
    mask_t = jnp.asarray(same.astype(np.float32))
    pd, pt = jnp.asarray(hot_d, BF), jnp.asarray(hot_t, BF)
    pdt, ptt = jnp.asarray(hot_d.T.copy(), BF), jnp.asarray(hot_t.T.copy(), BF)

    base = tokens.reshape(own, width)
    og = out_grad.reshape(own, width)
    gain1 = first_gain.reshape(1, width)
    gain2 = second_gain.reshape(1, width)
    taps = spatial_kernel.reshape(27, hid)

    send_d, send_t = pl.pallas_call(
        first_kernel,
        out_shape=(shape((rows_d, width), BF), shape((rows_t, width), BF)),
        in_specs=[VM] * 4,
        out_specs=(VM, VM),
        compiler_params=params(),
        name="first_norm",
    )(base, gain1, pd, pt)
    xd, xt = exchange(send_d, send_t, nd, nt)

    def trio(rows):
        return (
            shape((rows, 3 * width), BF),
            shape((width, rows), BF),
            shape((rows, width), BF),
        )

    def trio_scratch(rows):
        return [
            pltpu.VMEM((width, rows), F32),
            pltpu.VMEM((rows, width), F32),
            pltpu.VMEM((width, rows), BF),
        ]

    fields_d, mixed_d, branch_d, fields_t, mixed_t, branch_t = pl.pallas_call(
        attention_kernel,
        out_shape=trio(rows_d) + trio(rows_t),
        in_specs=[SM, SM] + [VM] * 8,
        out_specs=(VM,) * 6,
        scratch_shapes=trio_scratch(rows_d) + trio_scratch(rows_t),
        compiler_params=params(),
        name="attention",
    )(
        depth_scale, time_scale, xd, xt, depth_qkv, depth_out, time_qkv, time_out, mask_d, mask_t
    )
    bd, bt = exchange(branch_d, branch_t, nd, nt)
    middle = pl.pallas_call(
        middle_kernel,
        out_shape=shape((own, width), BF),
        in_specs=[VM] * 5,
        out_specs=VM,
        compiler_params=params(),
        name="middle",
    )(base, bd, bt, pdt, ptt)

    forward = [(i, i + 1) for i in range(nd - 1)]
    backward = [(target, source) for source, target in forward]
    low = lax.ppermute(middle[own - cells :], "dev", forward)
    high = lax.ppermute(middle[:cells], "dev", backward)

    def whole(dims):
        return pl.BlockSpec(dims, lambda c: (0, 0))

    def across(rows):
        return pl.BlockSpec((rows, CHUNK), lambda c: (0, c))

    def down_spec():
        return pl.BlockSpec((CHUNK, width), lambda c: (c, 0))

    fg, block_out, down_grad, kernel_grad, normed = pl.pallas_call(
        functools.partial(feed_kernel, factor, slabs, cells),
        grid=(hid // CHUNK,),
        out_shape=(
            shape((own, hid), BF),
            shape((own, width), BF),
            shape((hid, width), BF),
            shape((27, hid), F32),
            shape((own, width), BF),
        ),
        in_specs=[
            whole((cells, width)),
            whole((own, width)),
            whole((cells, width)),
            whole((1, width)),
            whole((own, width)),
            across(width),
            across(27),
            down_spec(),
        ],
        out_specs=(
            across(own),
            whole((own, width)),
            down_spec(),
            across(27),
            whole((own, width)),
        ),
        scratch_shapes=[
            pltpu.VMEM((own + 2 * cells, width), BF),
            pltpu.VMEM((3, slabs + 2, cells + 2 * PW, CHUNK), F32),
            pltpu.VMEM((own, width), F32),
            pltpu.VMEM((own, CHUNK), BF),
        ],
        compiler_params=params(dimension_semantics=("arbitrary",)),
        name="feed",
    )(low, middle, high, gain2, og, up_weight, taps, down_weight)

    fg_low = lax.ppermute(fg[own - cells :], "dev", forward)
    fg_high = lax.ppermute(fg[:cells], "dev", backward)

    up_grad, middle_grad, gsend_d, gsend_t, gain2_grad = pl.pallas_call(
        functools.partial(feed_back_kernel, factor, slabs, cells),
        grid=(hid // CHUNK,),
        out_shape=(
            shape((width, hid), BF),
            shape((own, width), F32),
            shape((rows_d, width), BF),
            shape((rows_t, width), BF),
            shape((1, width), F32),
        ),
        in_specs=[
            across(cells),
            across(own),
            across(cells),
            across(27),
            across(width),
            whole((own, width)),
            whole((own, width)),
            whole((own, width)),
            whole((1, width)),
            whole((rows_d, own)),
            whole((rows_t, own)),
        ],
        out_specs=(
            across(width),
            whole((own, width)),
            whole((rows_d, width)),
            whole((rows_t, width)),
            whole((1, width)),
        ),
        scratch_shapes=[
            pltpu.VMEM((3, slabs + 2, cells + 2 * PW, CHUNK), F32),
            pltpu.VMEM((width, own), BF),
            pltpu.VMEM((own, width), F32),
            pltpu.VMEM((own, CHUNK), BF),
        ],
        compiler_params=params(dimension_semantics=("arbitrary",)),
        name="feed_back",
    )(fg_low, fg, fg_high, taps, up_weight, normed, middle, og, gain2, pd, pt)

    gd, gt = exchange(gsend_d, gsend_t, nd, nt)

    def back_scratch(rows):
        return [
            pltpu.VMEM((width, rows), F32),
            pltpu.VMEM((width, rows), F32),
            pltpu.VMEM((width, rows), BF),
            pltpu.VMEM((rows, 3 * width), F32),
            pltpu.VMEM((width, rows), F32),
            pltpu.VMEM((rows, 3 * width), F32),
        ]

    (
        first_d, first_t, dqkv_grad, tqkv_grad, dout_grad, tout_grad, dsg, tsg,
    ) = pl.pallas_call(
        functools.partial(attention_back_kernel, factor),
        out_shape=(
            shape((rows_d, width), BF),
            shape((rows_t, width), BF),
            shape((width, 3 * width), BF),
            shape((width, 3 * width), BF),
            shape((width, width), BF),
            shape((width, width), BF),
            shape((heads, rows_d), F32),
            shape((heads, rows_t), F32),
        ),
        in_specs=[SM, SM] + [VM] * 14,
        out_specs=(VM,) * 8,
        scratch_shapes=back_scratch(rows_d) + back_scratch(rows_t),
        compiler_params=params(),
        name="attention_back",
    )(
        depth_scale, time_scale, xd, xt, gd, gt, fields_d, fields_t, mixed_d, mixed_t,
        depth_qkv, depth_out, time_qkv, time_out, mask_d, mask_t,
    )
    fd, ft = exchange(first_d, first_t, nd, nt)
    input_grad, gain1_grad = pl.pallas_call(
        last_kernel,
        out_shape=(shape((own, width), BF), shape((1, width), F32)),
        in_specs=[VM] * 7,
        out_specs=(VM, VM),
        compiler_params=params(),
        name="last_norm",
    )(base, gain1, fd, ft, pdt, ptt, middle_grad)

    axes = ("dev", "ta")
    down_sum = lax.psum(down_grad, axes)
    up_sum = lax.psum(up_grad, axes)
    dqkv_sum, tqkv_sum, dout_sum, tout_sum = lax.psum(
        (dqkv_grad, tqkv_grad, dout_grad, tout_grad), axes
    )
    small = jnp.concatenate(
        [
            kernel_grad.reshape(-1),
            gain1_grad.reshape(-1) * factor,
            gain2_grad.reshape(-1) * factor,
            jnp.sum(dsg, axis=1) * factor,
            jnp.sum(tsg, axis=1) * factor,
        ]
    )
    small = lax.psum(small, axes)
    at = 27 * hid
    return (
        block_out.reshape(tokens.shape),
        input_grad.reshape(tokens.shape),
        dqkv_sum.astype(F32),
        dout_sum.astype(F32),
        tqkv_sum.astype(F32),
        tout_sum.astype(F32),
        up_sum.astype(F32),
        small[:at].reshape(spatial_kernel.shape),
        down_sum.astype(F32),
        small[at : at + width],
        small[at + width : at + 2 * width],
        small[at + 2 * width : at + 2 * width + heads],
        small[at + 2 * width + heads :],
    )


def solution(mesh):
    lead = P("ta", "dev", None, None)
    return jax.shard_map(
        local,
        mesh=mesh,
        in_specs=(lead, lead) + (P(),) * 11,
        out_specs=(lead, lead) + (P(),) * 11,
        check_vma=False,
    )
```

time: 489 us -> 450 us (0.920); the launches traced: 479 us -> 449 us
  waiting for transfers between devices: 151 us -> 279 us
  Pallas kernels: 0 us -> 124 us
  local copies, waits for them, and re-layouts: 85.5 us -> 11.5 us
  matrix products: 63.3 us -> 0 us
  other arithmetic: 64.3 us -> 11.3 us
  blocking collectives: 52.5 us -> 0 us
  starting transfers between devices: 45.9 us -> 9.25 us
    psum x1 -> x2, waiting for transfers between devices: 125 us -> 274 us  [the longest x1 152 us: local(): lax.psum((dqkv_grad, tqkv_grad, dout_grad, tout_grad), axes)]
    pallas_call x0 -> x11, Pallas kernels: none -> 124 us  [the longest x4 57.4 us: exchange(): pl.pallas_call(functools.partial(exchange_kernel, nd, nt), out_shape=(jax...]
    dot_general x30 -> x0, matrix products: 63.3 us -> none  [the longest x6 21.5 us: attend(): jnp.einsum('plbhd,pmbhd->pbhlm', query, keyed, precision=lax.Precision.HI...]
    psum x1 -> x0, blocking collectives: 40.8 us -> none  [local(): lax.psum((depth_qkv_grad, depth_out_grad, time_qkv_grad, time_out_grad, u...]
    all_to_all x7 -> x0, starting transfers between devices: 30.7 us -> none  [the longest x1 5.09 us: local(): lax.all_to_all(rounded(project(time_regroup, time_out)), 'ta', split_axis...]
    another operation x30 -> x0, local copies, waits for them, and re-layouts: 25.2 us -> none  [the longest x28 22 us: kernel_terms(): return jnp.stack(terms).reshape(3, 3, 3, grads.shape[4])]
    all_to_all x7 -> x0, waiting for transfers between devices: 23.6 us -> none  [the longest x1 8.07 us: local(): lax.all_to_all(rounded(back_project(depth_fields_grad, depth_qkv)), 'dev'...]
    mul x18 -> x3, other arithmetic: 17.4 us -> 0.72 us  [the longest x1 0.7 us: local(): gain1_grad.reshape(-1) * factor]
  transfers between devices with their start and end apart: 12 -> 6, of which waited for: 6 -> 4; matrix products, arithmetic and copies ran while one was open for 27% -> 1% of each run, Pallas kernels for 0% -> 0%
where the time goes in v1:
time: 450 us; the launch traced here: 449 us
  waiting for transfers between devices  279 us (62%)
  Pallas kernels  124 us (28%)
  between operations  14.2 us (3%)
  local copies, waits for them, and re-layouts  11.5 us (3%)
  other arithmetic  11.3 us (3%)
  starting transfers between devices  9.25 us (2%)
    psum x1, waiting for transfers between devices, local(): lax.psum((dqkv_grad, tqkv_grad, dout_grad, tout_grad), axes)  152 us
    psum x1, waiting for transfers between devices, local(): small = lax.psum(small, axes)  122 us
    pallas_call x4, Pallas kernels, exchange(): pl.pallas_call(functools.partial(exchange_kernel, nd, nt), out_shape=(jax...  57.4 us
    pallas_call x1, Pallas kernels, local(): pl.pallas_call(functools.partial(attention_back_kernel, factor), out_shap...  21.3 us
    pallas_call x1, Pallas kernels, local(): pl.pallas_call(functools.partial(feed_kernel, factor, slabs, cells), grid...  16.3 us
    pallas_call x1, Pallas kernels, local(): pl.pallas_call(attention_kernel, out_shape=trio(rows_d) + trio(rows_t), i...  11.2 us
    pallas_call x1, Pallas kernels, local(): pl.pallas_call(functools.partial(feed_back_kernel, factor, slabs, cells),...  10.4 us
  transfers between devices with their start and end apart: 6, of which 4 were waited for; matrix products, arithmetic and copies ran while one was open for 1% of the time, Pallas kernels for 0%

profile of v1, /device:TPU:0, one launch (start us, length us, event | category | flops | bytes accessed | tf_op | source)
XLA Modules:
  0.0 449.4 jit_solution(10103262740377616088)
XLA Ops:
  7.2 1.2 reshape.108.gain
  8.5 2.6 first_norm.1
  11.1 14.8 %exchange.4 = (bf16[8,48,384]{2,1,0:T(8,128)(2,1)}, bf16[4,96,384]{2,1,0:T(8,128)(2,1)}) custom-call(bf16[8,48,384]{2,1,0:T(8,128)(2,1)} %bitcast.35, bf16[4,96,384]{2,1,0:T(8,128)(2,1)} %bitcast.36), custom_call_target="tpu_custom_call" | custom-call | tf_op jit(solution)/shard_map/exchange/pallas_call | solution.py:104
  25.9 11.2 %attention.1 = (bf16[384,1152]{1,0:T(8,128)(2,1)}, bf16[384,384]{1,0:T(8,128)(2,1)}, bf16[384,384]{1,0:T(8,128)(2,1)}, bf16[384,1152]{1,0:T(8,128)(2,1)}, bf16[3...) custom-call(f32[6]{0:T(128)} %scale_d.3, f32[6]{0:T(128)} %scale_t.3, bf16[384,384]{1,0:T(8,128)(2,1)} %bitcast.23, ...), custom_call_target="tpu_custom_call" | custom-call | tf_op jit(solution)/shard_map/attention/pallas_call | solution.py:475
  37.1 10.8 %exchange.5 = (bf16[8,48,384]{2,1,0:T(8,128)(2,1)}, bf16[4,96,384]{2,1,0:T(8,128)(2,1)}) custom-call(bf16[8,48,384]{2,1,0:T(8,128)(2,1)} %bitcast.33, bf16[4,96,384]{2,1,0:T(8,128)(2,1)} %bitcast.34), custom_call_target="tpu_custom_call" | custom-call | tf_op jit(solution)/shard_map/exchange/pallas_call | solution.py:104
  47.9 2.4 middle.1.mid
  50.4 1.0 fusion.1
  51.3 1.3 collective-permute-start
  52.6 1.3 collective-permute-start.1
  55.3 1.8 collective-permute-done.1.high
  57.7 16.3 %feed.1 = (bf16[288,1536]{1,0:T(8,128)(2,1)}, bf16[288,384]{1,0:T(8,128)(2,1)}, bf16[1536,384]{1,0:T(8,128)(2,1)}, f32[27,1536]{1,0:T(8,128)}, bf16[288,384]{1,0:T(8,128)(2,1)}) custom-call(bf16[144,384]{1,0:T(8,128)(2,1)} %copy-done.9, bf16[288,384]{1,0:T(8,128)(2,1)} %middle.1.mid, bf16[144,384]{1,0:T(8,128)(2,1)} %copy-done.10, f32[1,384]{1,0:T(1,128)} %reshape.117.gain, ...), custom_call_target="tpu_custom_call" | custom-call | tf_op jit(solution)/shard_map/feed/pallas_call | solution.py:510
  74.1 1.2 fusion
  75.4 5.3 %collective-permute-start.2 = (bf16[144,1536]{1,0:T(8,128)(2,1)S(1)}, bf16[144,1536]{1,0:T(8,128)(2,1)S(1)}, u32[]{:S(2)}, u32[]{:S(2)}) collective-permute-start(bf16[144,1536]{1,0:T(8,128)(2,1)S(1)} %get-tuple-element.92), channel_id=1, source_target_pairs={{0,4},{4,8},{8,12},{12,16},{16,20},{20,24},{24,28},{1,5},{5,9},{9,... | collective-permute-start | bytes 1327112 | tf_op jit(solution)/shard_map/ppermute | solution.py:547
  80.7 1.3 collective-permute-start.3
  82.0 2.3 collective-permute-done.3.high
  85.1 10.4 %feed_back.1 = (bf16[384,1536]{1,0:T(8,128)(2,1)}, f32[288,384]{1,0:T(8,128)}, bf16[384,384]{1,0:T(8,128)(2,1)}, bf16[384,384]{1,0:T(8,128)(2,1)}, f32[1,384]{1,0:T(1,128)}) custom-call(bf16[144,1536]{1,0:T(8,128)(2,1)} %copy-done.3, bf16[288,1536]{1,0:T(8,128)(2,1)} %get-tuple-element.58.fg, bf16[144,1536]{1,0:T(8,128)(2,1)} %copy-done.4, ...), custom_call_target="tpu_custom_call" | custom-call | tf_op jit(solution)/shard_map/feed_back/pallas_call | solution.py:550
  95.5 18.2 %exchange.6 = (bf16[8,48,384]{2,1,0:T(8,128)(2,1)}, bf16[4,96,384]{2,1,0:T(8,128)(2,1)}) custom-call(bf16[8,48,384]{2,1,0:T(8,128)(2,1)} %bitcast.31, bf16[4,96,384]{2,1,0:T(8,128)(2,1)} %bitcast.32), custom_call_target="tpu_custom_call" | custom-call | tf_op jit(solution)/shard_map/exchange/pallas_call | solution.py:104
  113.7 21.3 %attention_back.1 = (bf16[384,384]{1,0:T(8,128)(2,1)}, bf16[384,384]{1,0:T(8,128)(2,1)}, bf16[384,1152]{1,0:T(8,128)(2,1)}, bf16[384,1152]{1,0:T(8,128)(2,1)}, b...) custom-call(f32[6]{0:T(128)} %scale_d.3, f32[6]{0:T(128)} %scale_t.3, ...), custom_call_target="tpu_custom_call" | custom-call | tf_op jit(solution)/shard_map/attention_back/pallas_call | solution.py:604
  135.0 0.8 reduce_sum.18
  136.6 13.6 %exchange.7 = (bf16[8,48,384]{2,1,0:T(8,128)(2,1)}, bf16[4,96,384]{2,1,0:T(8,128)(2,1)}) custom-call(bf16[8,48,384]{2,1,0:T(8,128)(2,1)} %bitcast.29, bf16[4,96,384]{2,1,0:T(8,128)(2,1)} %bitcast.30), custom_call_target="tpu_custom_call" | custom-call | tf_op jit(solution)/shard_map/exchange/pallas_call | solution.py:104
  150.2 2.8 last_norm.1
  155.2 121.5 %all-reduce.4.cloned.1.call-done = f32[42252]{0:T(1024)} async-done(((f32[42252]{0:T(1024)}), f32[42252]{0:T(1024)}) %all-reduce.4.cloned.1.call-update) | async-done | bytes 169024 | tf_op jit(solution)/shard_map/psum | solution.py:650
  276.7 0.9 slice.38
  278.4 1.3 fusion.2
  279.8 1.3 fusion.3
  281.1 152.3 %all-reduce.6.cloned.1.call-done = (bf16[384,1152]{1,0:T(8,128)(2,1)}, bf16[384,384]{1,0:T(8,128)(2,1)}, bf16[384,1152]{1,0:T(8,128)(2,1)}, bf16[384,384]{1,0:T(...) async-done(((bf16[384,1152]{1,0:T(8,128)(2,1)}, bf16[384,384]{1,0:T(8,128)(2,1)}, bf16[384,1152]{1,0:T(8,128)(2,1)}, bf16[384,384]{1,0:T(8,128)(2,1)}, ...) | async-done | bytes 4718608 | tf_op jit(solution)/shard_map/psum | solution.py:638
  433.4 3.1 convert_element_type.22
  436.4 1.6 convert_element_type.23
  438.0 1.3 convert_element_type.18
  439.5 1.3 convert_element_type.20
  440.8 0.9 convert_element_type.19
  441.7 0.9 convert_element_type.21
  (41 shorter events, 6.8 us)
Async XLA Ops:
  7.2 269.6 %all-reduce.4.cloned.1.call-start = ((), (), s32[]{:S(2)}) async-start(), calls=%async_computation | async-start | bytes 344064 | tf_op jit(solution)/shard_map/psum | solution.py:650
  37.1 16.9 %copy-start.7 = (f32[3,3,3,1536]{3,2,1,0:T(4,128)S(1)}, f32[3,3,3,1536]{3,2,1,0:T(4,128)}, u32[]{:S(2)}) copy-start(f32[3,3,3,1536]{3,2,1,0:T(4,128)} %param.28) | copy-start | bytes 497668
  47.9 6.8 %copy-start.11 = (f32[384]{0:T(512)S(1)}, f32[384]{0:T(512)}, u32[]{:S(2)}) copy-start(f32[384]{0:T(512)} %param.26) | copy-start | bytes 4612
  51.3 3.9 collective-permute-start
  52.6 4.5 collective-permute-start.1
  55.3 1.8 copy-start.9
  57.1 0.6 copy-start.10
  74.1 7.9 %copy-start.8 = (f32[27,1536]{1,0:T(8,128)S(1)}, f32[27,1536]{1,0:T(8,128)}, u32[]{:S(2)}) copy-start(f32[27,1536]{1,0:T(8,128)} %get-tuple-element.79) | copy-start | bytes 497668
  75.4 6.7 %collective-permute-start.2 = (bf16[144,1536]{1,0:T(8,128)(2,1)S(1)}, bf16[144,1536]{1,0:T(8,128)(2,1)S(1)}, u32[]{:S(2)}, u32[]{:S(2)}) collective-permute-start(bf16[144,1536]{1,0:T(8,128)(2,1)S(1)} %get-tuple-element.92), channel_id=1, source_target_pairs={{0,4},{4,8},{8,12},{12,16},{16,20},{20,24},{24,28},{1,5},{5,9},{9,... | collective-permute-start | bytes 1327112 | tf_op jit(solution)/shard_map/ppermute | solution.py:547
  80.7 3.7 collective-permute-start.3
  82.0 2.3 copy-start.3
  84.3 0.8 copy-start.4
  134.9 18.7 %copy-start.12 = (f32[1,384]{1,0:T(1,128)S(1)}, f32[1,384]{1,0:T(1,128)}, u32[]{:S(2)}) copy-start(f32[1,384]{1,0:T(1,128)} %get-tuple-element.81) | copy-start | bytes 4612
  154.5 278.9 %all-reduce.6.cloned.1.call-start = ((), (), s32[]{:S(2)}) async-start(), calls=%async_computation.1 | async-start | bytes 9437184 | tf_op jit(solution)/shard_map/psum | solution.py:638
  433.4 3.1 copy-start
  436.4 1.6 copy-start.2
  438.0 1.5 copy-start.1
  439.5 1.3 copy-start.6
  439.5 2.2 copy-start.5
Sparse Core Ops, SparseCore 0:
  154.6 122.0 all-reduce.3
  283.7 149.5 all-reduce.5

commit v2 on v1

--- a/solution.py
+++ b/solution.py
@@ -53,17 +53,20 @@
     return part * inverse, jnp.sum(back * high, axis=0, keepdims=True)
 
 
-def exchange_kernel(nd, nt, sd, st, rd, rt, send_d, recv_d, send_t, recv_t):
+def greet(barrier, nd, nt):
     d = lax.axis_index("dev")
     t = lax.axis_index("ta")
-    barrier = pltpu.get_barrier_semaphore()
     for off in range(1, nd):
         peer = lax.rem(d + off, nd)
         pl.semaphore_signal(barrier, inc=1, device_id=(peer, t), device_id_type=MESH)
     for off in range(1, nt):
         peer = lax.rem(t + off, nt)
         pl.semaphore_signal(barrier, inc=1, device_id=(d, peer), device_id_type=MESH)
-    pl.semaphore_wait(barrier, nd + nt - 2)
+
+
+def block_copies(nd, nt, sd, st, rd, rt, send_d, recv_d, send_t, recv_t):
+    d = lax.axis_index("dev")
+    t = lax.axis_index("ta")
     copies = []
     for off in range(1, nt):
         peer = lax.rem(t + off, nt)
@@ -89,10 +92,18 @@
                 device_id_type=MESH,
             )
         )
+    return copies
+
+
+def exchange_kernel(nd, nt, sd, st, rd, rt, *sems):
+    barrier = pltpu.get_barrier_semaphore()
+    greet(barrier, nd, nt)
+    pl.semaphore_wait(barrier, nd + nt - 2)
+    copies = block_copies(nd, nt, sd, st, rd, rt, *sems)
     for copy in copies:
         copy.start()
-    rd[d] = sd[d]
-    rt[t] = st[t]
+    rd[lax.axis_index("dev")] = sd[lax.axis_index("dev")]
+    rt[lax.axis_index("ta")] = st[lax.axis_index("ta")]
     for copy in copies:
         copy.wait()
 
@@ -170,7 +181,7 @@
 
 def attend_backward(
     x, grads, fields, mixed_t, qkv, out, mask, scale, factor,
-    first, qkv_grad, out_grad, scale_grad, qt, kt, gt, natural, dqt, dfields,
+    first, qkv_grad, out_grad, scale_grad, gains, qt, kt, gt, natural, dqt, dfields,
 ):
     rows, width = x.shape
     heads = scale.shape[0]
@@ -232,7 +243,9 @@
         dfields[:, width + lo : width + hi] = back * inverse_k
     dfields[:, :width] = dqt[...].T
     narrow = dfields[...].astype(BF)
-    first[...] = dot_nt(narrow, qkv[...]).astype(BF)
+    back = dot_nt(narrow, qkv[...]).astype(BF)
+    first[...] = back
+    gains[...] += jnp.sum(back.astype(F32) * x[...].astype(F32), axis=0, keepdims=True)
     turned = x[...].astype(F32).T.astype(BF)
     qkv_grad[...] = (dot(turned, narrow) * factor).astype(BF)
 
@@ -240,15 +253,16 @@
 def attention_back_kernel(
     factor, scale_d, scale_t, xd, xt, gd, gt_, fields_d, fields_t, mixed_d, mixed_t,
     qkv_d, out_d, qkv_t, out_t, mask_d, mask_t,
-    first_d, first_t, qkv_grad_d, qkv_grad_t, out_grad_d, out_grad_t, sg_d, sg_t, *scratch,
+    first_d, first_t, qkv_grad_d, qkv_grad_t, out_grad_d, out_grad_t, sg_d, sg_t, gains, *scratch,
 ):
+    gains[...] = jnp.zeros_like(gains)
     attend_backward(
         xd, gd, fields_d, mixed_d, qkv_d, out_d, mask_d, scale_d, factor,
-        first_d, qkv_grad_d, out_grad_d, sg_d, *scratch[:6],
+        first_d, qkv_grad_d, out_grad_d, sg_d, gains, *scratch[:6],
     )
     attend_backward(
         xt, gt_, fields_t, mixed_t, qkv_t, out_t, mask_t, scale_t, factor,
-        first_t, qkv_grad_t, out_grad_t, sg_t, *scratch[6:],
+        first_t, qkv_grad_t, out_grad_t, sg_t, gains, *scratch[6:],
     )
 
 
@@ -386,11 +400,199 @@
         send_t[...] = dot(pt[...], narrow).astype(BF)
 
 
-def last_kernel(tokens, gain, fd, ft, pdt, ptt, middle_grad, input_grad, gain_grad):
+def last_kernel(tokens, gain, fd, ft, pdt, ptt, middle_grad, input_grad):
     back = dot(pdt[...], fd[...]) + dot(ptt[...], ft[...])
-    part, gains = norm_back(tokens[...].astype(F32), gain[...], back)
-    gain_grad[...] = gains
+    part, _ = norm_back(tokens[...].astype(F32), gain[...], back)
     input_grad[...] = (middle_grad[...] + part).astype(BF)
+
+
+def bits_of(count):
+    assert count & (count - 1) == 0
+    return count.bit_length() - 1
+
+
+def orders_of(nd, nt):
+    dev = [("dev", bit) for bit in range(bits_of(nd))]
+    time = [("ta", bit) for bit in range(bits_of(nt))]
+    head, near, far = dev[:1], dev[1:2], dev[2:]
+    return (head + near + far + time, head + far + time + near, head + time + near + far)
+
+
+def pack_plan(width, hid):
+    blocks = [3, 3, 1, 1, hid // width]
+    plan, at = [], 0
+    for array, count in enumerate(blocks):
+        for block in range(count):
+            plan.append((array, block, at))
+            at += width
+    return plan, at
+
+
+def sum_kernel(
+    nd, nt, plan, at_down, qd, qt, od, ot, up, down, small, sd, st,
+    big_out, small_out, rd, rt, big_sum, small_sum, big_in, small_in, send_sem, recv_sem, *sems,
+):
+    place = {"dev": lax.axis_index("dev"), "ta": lax.axis_index("ta")}
+    orders = orders_of(nd, nt)
+    stages = len(orders[0])
+    width = down.shape[1]
+
+    def digit(axis, bit):
+        return lax.rem(place[axis] // (1 << bit), 2)
+
+    def partner(axis, bit):
+        moved = place[axis] + (1 - 2 * digit(axis, bit)) * (1 << bit)
+        if axis == "dev":
+            return (moved, place["ta"])
+        return (place["dev"], moved)
+
+    barrier = pltpu.get_barrier_semaphore()
+    greet(barrier, nd, nt)
+
+    arrays = (qd, qt, od, ot, up)
+    for array, block, at in plan:
+        big_sum[at : at + width, :] = arrays[array][:, block * width : (block + 1) * width]
+    big_sum[at_down:, :] = down[...]
+    small_sum[...] = small[...]
+    rd[place["dev"]] = sd[place["dev"]]
+    rt[place["ta"]] = st[place["ta"]]
+    pl.semaphore_wait(barrier, nd + nt - 2)
+    blocks = block_copies(nd, nt, sd, st, rd, rt, *sems)
+    for copy in blocks:
+        copy.start()
+
+    each = big_out.shape[0] // 3
+    parts = []
+    for index, order in enumerate(orders):
+        parts.append((big_sum, big_out, big_in, order, index * each, each, 16))
+    parts.append((small_sum, small_out, small_in, orders[1], 0, small_out.shape[0], 8))
+
+    spans = []
+    for target, result, landing, order, base, size, unit in parts:
+        offs, sizes = [base], [size]
+        for axis, bit in order:
+            sizes.append(sizes[-1] // 2)
+            offs.append(offs[-1] + digit(axis, bit) * sizes[-1])
+        spans.append((offs, sizes))
+
+    def reduce_copy(index, stage):
+        target, result, landing, order, base, size, unit = parts[index]
+        offs, sizes = spans[index]
+        axis, bit = order[stage]
+        half = sizes[stage + 1]
+        away = offs[stage] + (1 - digit(axis, bit)) * half
+        to = base + size - sizes[stage]
+        return pltpu.make_async_remote_copy(
+            src_ref=target.at[pl.ds(pl.multiple_of(away, unit), half), :],
+            dst_ref=landing.at[pl.ds(to, half), :],
+            send_sem=send_sem.at[index, stage],
+            recv_sem=recv_sem.at[index, stage],
+            device_id=partner(axis, bit),
+            device_id_type=MESH,
+        )
+
+    def gather_copy(index, stage):
+        target, result, landing, order, base, size, unit = parts[index]
+        offs, sizes = spans[index]
+        axis, bit = order[stage]
+        rows = pl.ds(pl.multiple_of(offs[stage + 1], unit), sizes[stage + 1])
+        return pltpu.make_async_remote_copy(
+            src_ref=result.at[rows, :],
+            dst_ref=result.at[rows, :],
+            send_sem=send_sem.at[index, stages + stage],
+            recv_sem=recv_sem.at[index, stages + stage],
+            device_id=partner(axis, bit),
+            device_id_type=MESH,
+        )
+
+    count = len(parts)
+    flying = []
+    for index in range(count):
+        copy = reduce_copy(index, 0)
+        copy.start()
+        flying.append(copy)
+    for stage in range(stages):
+        for index in range(count):
+            flying[index].wait()
+            target, result, landing, order, base, size, unit = parts[index]
+            offs, sizes = spans[index]
+            half = sizes[stage + 1]
+            to = base + size - sizes[stage]
+            rows = pl.ds(pl.multiple_of(offs[stage + 1], unit), half)
+            added = target[rows, :].astype(F32) + landing[to : to + half, :].astype(F32)
+            if stage + 1 < stages:
+                target[rows, :] = added.astype(target.dtype)
+                copy = reduce_copy(index, stage + 1)
+            else:
+                result[rows, :] = added.astype(result.dtype)
+                copy = gather_copy(index, stages - 1)
+            copy.start()
+            flying[index] = copy
+    for stage in range(stages - 1, -1, -1):
+        for index in range(count):
+            flying[index].wait()
+            if stage > 0:
+                copy = gather_copy(index, stage - 1)
+                copy.start()
+                flying[index] = copy
+    for copy in blocks:
+        copy.wait()
+
+
+def unpack_kernel(plan, at_down, big, qd, qt, od, ot, up, down):
+    width = down.shape[1]
+    arrays = (qd, qt, od, ot, up)
+    for array, block, at in plan:
+        arrays[array][:, block * width : (block + 1) * width] = big[at : at + width, :].astype(F32)
+    down[...] = big[at_down:, :].astype(F32)
+
+
+def sum_all(qd, qt, od, ot, up, down, small, send_d, send_t, nd, nt):
+    width, hid = up.shape
+    plan, at_down = pack_plan(width, hid)
+    rows = at_down + hid
+    devices = nd * nt
+    stages = bits_of(devices)
+    assert rows % (3 * 16 * devices) == 0
+    unit = 8 * devices
+    small_rows = -(-small.shape[0] // (unit * width)) * unit
+    small = jnp.pad(small, (0, small_rows * width - small.shape[0])).reshape(small_rows, width)
+    sd = send_d.reshape(nd, -1, width)
+    st = send_t.reshape(nt, -1, width)
+    big, small, rd, rt = pl.pallas_call(
+        functools.partial(sum_kernel, nd, nt, plan, at_down),
+        out_shape=(
+            shape((rows, width), BF),
+            shape((small_rows, width), F32),
+            shape(sd.shape, BF),
+            shape(st.shape, BF),
+        ),
+        in_specs=[VM] * 9,
+        out_specs=(VM,) * 4,
+        scratch_shapes=[
+            pltpu.VMEM((rows, width), BF),
+            pltpu.VMEM((small_rows, width), F32),
+            pltpu.VMEM((rows, width), BF),
+            pltpu.VMEM((small_rows, width), F32),
+            pltpu.SemaphoreType.DMA((4, 2 * stages)),
+            pltpu.SemaphoreType.DMA((4, 2 * stages)),
+            pltpu.SemaphoreType.DMA((nd - 1,)),
+            pltpu.SemaphoreType.DMA((nd - 1,)),
+            pltpu.SemaphoreType.DMA((nt - 1,)),
+            pltpu.SemaphoreType.DMA((nt - 1,)),
+        ],
+        compiler_params=params(collective_id=1, has_side_effects=True),
+        name="sum_all",
+    )(qd, qt, od, ot, up, down, small, sd, st)
+    wide = pl.pallas_call(
+        functools.partial(unpack_kernel, plan, at_down),
+        out_shape=tuple(shape(value.shape, F32) for value in (qd, qt, od, ot, up, down)),
+        in_specs=[VM],
+        out_specs=(VM,) * 6,
+        compiler_params=params(),
+        name="unpack",
+    )(big)
+    return wide, small.reshape(-1), rd.reshape(send_d.shape), rt.reshape(send_t.shape)
 
 
 def placement(groups, slabs, cells):
@@ -600,7 +802,7 @@
         ]
 
     (
-        first_d, first_t, dqkv_grad, tqkv_grad, dout_grad, tout_grad, dsg, tsg,
+        first_d, first_t, dqkv_grad, tqkv_grad, dout_grad, tout_grad, dsg, tsg, gain1_part,
     ) = pl.pallas_call(
         functools.partial(attention_back_kernel, factor),
         out_shape=(
@@ -612,9 +814,10 @@
             shape((width, width), BF),
             shape((heads, rows_d), F32),
             shape((heads, rows_t), F32),
+            shape((1, width), F32),
         ),
         in_specs=[SM, SM] + [VM] * 14,
-        out_specs=(VM,) * 8,
+        out_specs=(VM,) * 9,
         scratch_shapes=back_scratch(rows_d) + back_scratch(rows_t),
         compiler_params=params(),
         name="attention_back",
@@ -622,47 +825,44 @@
         depth_scale, time_scale, xd, xt, gd, gt, fields_d, fields_t, mixed_d, mixed_t,
         depth_qkv, depth_out, time_qkv, time_out, mask_d, mask_t,
     )
-    fd, ft = exchange(first_d, first_t, nd, nt)
-    input_grad, gain1_grad = pl.pallas_call(
-        last_kernel,
-        out_shape=(shape((own, width), BF), shape((1, width), F32)),
-        in_specs=[VM] * 7,
-        out_specs=(VM, VM),
-        compiler_params=params(),
-        name="last_norm",
-    )(base, gain1, fd, ft, pdt, ptt, middle_grad)
-
-    axes = ("dev", "ta")
-    down_sum = lax.psum(down_grad, axes)
-    up_sum = lax.psum(up_grad, axes)
-    dqkv_sum, tqkv_sum, dout_sum, tout_sum = lax.psum(
-        (dqkv_grad, tqkv_grad, dout_grad, tout_grad), axes
-    )
     small = jnp.concatenate(
         [
             kernel_grad.reshape(-1),
-            gain1_grad.reshape(-1) * factor,
+            gain1_part.reshape(-1) / first_gain * factor,
             gain2_grad.reshape(-1) * factor,
             jnp.sum(dsg, axis=1) * factor,
             jnp.sum(tsg, axis=1) * factor,
         ]
     )
-    small = lax.psum(small, axes)
+    grads, small, fd, ft = sum_all(
+        dqkv_grad, tqkv_grad, dout_grad, tout_grad, up_grad, down_grad, small,
+        first_d, first_t, nd, nt,
+    )
+    input_grad = pl.pallas_call(
+        last_kernel,
+        out_shape=shape((own, width), BF),
+        in_specs=[VM] * 7,
+        out_specs=VM,
+        compiler_params=params(),
+        name="last_norm",
+    )(base, gain1, fd, ft, pdt, ptt, middle_grad)
+
+    dqkv_sum, tqkv_sum, dout_sum, tout_sum, up_sum, down_sum = grads
     at = 27 * hid
     return (
         block_out.reshape(tokens.shape),
         input_grad.reshape(tokens.shape),
-        dqkv_sum.astype(F32),
-        dout_sum.astype(F32),
-        tqkv_sum.astype(F32),
-        tout_sum.astype(F32),
-        up_sum.astype(F32),
+        dqkv_sum,
+        dout_sum,
+        tqkv_sum,
+        tout_sum,
+        up_sum,
         small[:at].reshape(spatial_kernel.shape),
-        down_sum.astype(F32),
+        down_sum,
         small[at : at + width],
         small[at + width : at + 2 * width],
         small[at + 2 * width : at + 2 * width + heads],
-        small[at + 2 * width + heads :],
+        small[at + 2 * width + heads : at + 2 * width + 2 * heads],
     )
 
 

time: 450 us -> 220 us (0.49)
  waiting for transfers between devices: 279 us -> 1.32 us
  Pallas kernels: 124 us -> 193 us
  between operations: 14.2 us -> 0.86 us
  other arithmetic: 11.3 us -> 2.38 us
    psum x2 -> x0, waiting for transfers between devices: 274 us -> none  [the longest x1 152 us: local(): lax.psum((dqkv_grad, tqkv_grad, dout_grad, tout_grad), axes)]
    pallas_call x1 -> x3, Pallas kernels: 2.76 us -> 79.7 us  [the longest x1 70.8 us: sum_all(): pl.pallas_call(functools.partial(sum_kernel, nd, nt, plan, at_down), out_...]
    convert_element_type x6 -> x0, other arithmetic: 8.97 us -> none  [the longest x1 3.06 us: local(): up_sum.astype(F32)]
    pallas_call x4 -> x3, Pallas kernels: 57.4 us -> 48.6 us  [exchange(): pl.pallas_call(functools.partial(exchange_kernel, nd, nt), out_shape=(jax...]
  transfers between devices with their start and end apart: 6 -> 4, of which waited for: 4 -> 1; matrix products, arithmetic and copies ran while one was open for 1% -> 1% of each run, Pallas kernels for 0% -> 0%
where the time goes in v2:
time: 220 us; the launch traced here: 218 us
  Pallas kernels  193 us (88%)
  local copies, waits for them, and re-layouts  11.9 us (5%)
  starting transfers between devices  9.15 us (4%)
  other arithmetic  2.38 us (1%)
    pallas_call x1, Pallas kernels, sum_all(): pl.pallas_call(functools.partial(sum_kernel, nd, nt, plan, at_down), out_...  70.8 us
    pallas_call x3, Pallas kernels, exchange(): pl.pallas_call(functools.partial(exchange_kernel, nd, nt), out_shape=(jax...  48.6 us
    pallas_call x1, Pallas kernels, local(): pl.pallas_call(functools.partial(attention_back_kernel, factor), out_shap...  21.3 us
    pallas_call x1, Pallas kernels, local(): pl.pallas_call(functools.partial(feed_kernel, factor, slabs, cells), grid...  16.3 us
    pallas_call x1, Pallas kernels, local(): pl.pallas_call(attention_kernel, out_shape=trio(rows_d) + trio(rows_t), i...  11.2 us
    pallas_call x1, Pallas kernels, local(): pl.pallas_call(functools.partial(feed_back_kernel, factor, slabs, cells),...  10.4 us
    pallas_call x1, Pallas kernels, sum_all(): pl.pallas_call(functools.partial(unpack_kernel, plan, at_down), out_shape...  6.12 us
  transfers between devices with their start and end apart: 4, of which 1 were waited for; matrix products, arithmetic and copies ran while one was open for 1% of the time, Pallas kernels for 0%

profile of v2, /device:TPU:0, one launch (start us, length us, event | category | flops | bytes accessed | tf_op | source)
XLA Modules:
  0.0 218.1 jit_solution(7907200273244816896)
XLA Ops:
  0.6 1.2 reshape.118.gain
  1.9 2.6 %first_norm.1 = (bf16[384,384]{1,0:T(8,128)(2,1)}, bf16[384,384]{1,0:T(8,128)(2,1)}) custom-call(bf16[288,384]{1,0:T(8,128)(2,1)} %bitcast.20, f32[1,384]{1,0:T(1,128)} %reshape.118.gain, bf16[384,288]{1,0:T(8,128)(2,1)} %constant.21.clone.pd, bf16[384,288]{1,0:T(8,128)(2,1)} %constant.22.clone.pt), custom_call_target="tpu_custom_call" | custom-call | tf_op jit(solution)/shard_map/first_norm/pallas_call | solution.py:653
  4.5 14.8 %exchange.3 = (bf16[8,48,384]{2,1,0:T(8,128)(2,1)}, bf16[4,96,384]{2,1,0:T(8,128)(2,1)}) custom-call(bf16[8,48,384]{2,1,0:T(8,128)(2,1)} %bitcast.35, bf16[4,96,384]{2,1,0:T(8,128)(2,1)} %bitcast.36), custom_call_target="tpu_custom_call" | custom-call | tf_op jit(solution)/shard_map/exchange/pallas_call | solution.py:115
  19.3 11.2 %attention.1 = (bf16[384,1152]{1,0:T(8,128)(2,1)}, bf16[384,384]{1,0:T(8,128)(2,1)}, bf16[384,384]{1,0:T(8,128)(2,1)}, bf16[384,1152]{1,0:T(8,128)(2,1)}, bf16[3...) custom-call(f32[6]{0:T(128)} %scale_d.3, f32[6]{0:T(128)} %scale_t.3, bf16[384,384]{1,0:T(8,128)(2,1)} %bitcast.23, ...), custom_call_target="tpu_custom_call" | custom-call | tf_op jit(solution)/shard_map/attention/pallas_call | solution.py:677
  30.5 10.8 %exchange.4 = (bf16[8,48,384]{2,1,0:T(8,128)(2,1)}, bf16[4,96,384]{2,1,0:T(8,128)(2,1)}) custom-call(bf16[8,48,384]{2,1,0:T(8,128)(2,1)} %bitcast.33, bf16[4,96,384]{2,1,0:T(8,128)(2,1)} %bitcast.34), custom_call_target="tpu_custom_call" | custom-call | tf_op jit(solution)/shard_map/exchange/pallas_call | solution.py:115
  41.4 2.4 %middle.1.mid = bf16[288,384]{1,0:T(8,128)(2,1)} custom-call(bf16[288,384]{1,0:T(8,128)(2,1)} %bitcast.21, bf16[384,384]{1,0:T(8,128)(2,1)} %bitcast.39, bf16[384,384]{1,0:T(8,128)(2,1)} %bitcast.40, bf16[288,384]{1,0:T(8,128)(2,1)} %constant.23.clone.pdt, bf16[288,384]{1,0:T(8,128)(2,1)} %constant.24.clone.ptt), custom_call_target="tpu_custom_call" | custom-call | tf_op jit(solution)/shard_map/middle/pallas_call | solution.py:689
  43.8 1.0 fusion.2
  44.8 1.3 collective-permute-start.1
  46.1 3.0 %collective-permute-start = (bf16[144,384]{1,0:T(8,128)(2,1)S(1)}, bf16[144,384]{1,0:T(8,128)(2,1)S(1)}, u32[]{:S(2)}, u32[]{:S(2)}) collective-permute-start(bf16[144,384]{1,0:T(8,128)(2,1)S(1)} %get-tuple-element.106), channel_id=1, source_target_pairs={{0,4},{4,8},{8,12},{12,16},{16,20},{20,24},{24,28},{1,5},{5,9},{9,... | collective-permute-start | bytes 331784 | tf_op jit(solution)/shard_map/ppermute | solution.py:700
  49.7 0.8 reshape.129.kernel
  50.5 0.6 copy-done.4
  51.2 16.3 %feed.1 = (bf16[288,1536]{1,0:T(8,128)(2,1)}, bf16[288,384]{1,0:T(8,128)(2,1)}, bf16[1536,384]{1,0:T(8,128)(2,1)}, f32[27,1536]{1,0:T(8,128)}, bf16[288,384]{1,0:T(8,128)(2,1)}) custom-call(bf16[144,384]{1,0:T(8,128)(2,1)} %copy-done.5, bf16[288,384]{1,0:T(8,128)(2,1)} %middle.1.mid, bf16[144,384]{1,0:T(8,128)(2,1)} %copy-done.4, f32[1,384]{1,0:T(1,128)} %reshape.127.gain, ...), custom_call_target="tpu_custom_call" | custom-call | tf_op jit(solution)/shard_map/feed/pallas_call | solution.py:712
  67.5 1.2 fusion
  68.8 1.3 collective-permute-start.3
  70.1 3.5 %collective-permute-start.2 = (bf16[144,1536]{1,0:T(8,128)(2,1)S(1)}, bf16[144,1536]{1,0:T(8,128)(2,1)S(1)}, u32[]{:S(2)}, u32[]{:S(2)}) collective-permute-start(bf16[144,1536]{1,0:T(8,128)(2,1)S(1)} %get-tuple-element.102), channel_id=1, source_target_pairs={{0,4},{4,8},{8,12},{12,16},{16,20},{20,24},{24,28},{1,5},{5,9},{9,... | collective-permute-start | bytes 1327112 | tf_op jit(solution)/shard_map/ppermute | solution.py:749
  73.7 1.3 collective-permute-done.2.low
  75.0 0.8 copy-done.1
  75.7 10.4 %feed_back.1 = (bf16[384,1536]{1,0:T(8,128)(2,1)}, f32[288,384]{1,0:T(8,128)}, bf16[384,384]{1,0:T(8,128)(2,1)}, bf16[384,384]{1,0:T(8,128)(2,1)}, f32[1,384]{1,0:T(1,128)}) custom-call(bf16[144,1536]{1,0:T(8,128)(2,1)} %copy-done.1, bf16[288,1536]{1,0:T(8,128)(2,1)} %get-tuple-element.65.fg, bf16[144,1536]{1,0:T(8,128)(2,1)} %copy-done, ...), custom_call_target="tpu_custom_call" | custom-call | tf_op jit(solution)/shard_map/feed_back/pallas_call | solution.py:752
  86.1 22.9 %exchange.5 = (bf16[8,48,384]{2,1,0:T(8,128)(2,1)}, bf16[4,96,384]{2,1,0:T(8,128)(2,1)}) custom-call(bf16[8,48,384]{2,1,0:T(8,128)(2,1)} %bitcast.31, bf16[4,96,384]{2,1,0:T(8,128)(2,1)} %bitcast.32), custom_call_target="tpu_custom_call" | custom-call | tf_op jit(solution)/shard_map/exchange/pallas_call | solution.py:115
  109.0 21.3 %attention_back.1 = (bf16[384,384]{1,0:T(8,128)(2,1)}, bf16[384,384]{1,0:T(8,128)(2,1)}, bf16[384,1152]{1,0:T(8,128)(2,1)}, bf16[384,1152]{1,0:T(8,128)(2,1)}, b...) custom-call(f32[6]{0:T(128)} %scale_d.3, ...), custom_call_target="tpu_custom_call" | custom-call | tf_op jit(solution)/shard_map/attention_back/pallas_call | solution.py:806
  130.4 0.8 reduce_sum.18
  131.2 0.8 reduce_sum.19
  132.0 0.7 reduce
  132.9 0.8 reshape.137.small
  133.7 70.8 %sum_all.1 = (bf16[6144,384]{1,0:T(8,128)(2,1)}, f32[256,384]{1,0:T(8,128)}, bf16[8,48,384]{2,1,0:T(8,128)(2,1)}, bf16[4,96,384]{2,1,0:T(8,128)(2,1)}) custom-call(bf16[384,1152]{1,0:T(8,128)(2,1)} %get-tuple-element.75.qd, bf16[384,1152]{1,0:T(8,128)(2,1)} %get-tuple-element.76.qt, bf16[384,384]{1,0:T(8,128)(2,1)} %get-tuple-element.77.od, ...), custom_call_target="tpu_custom_call" | custom-call | tf_op jit(solution)/shard_map/sum_all/pallas_call | solution.py:562
  204.6 1.4 slice_reduce_fusion
  205.9 0.9 slice.38
  206.9 1.0 reshape.144
  207.9 0.6 fusion.1
  208.5 0.7 reshape.143
  209.2 6.1 %unpack.1 = (f32[384,1152]{1,0:T(8,128)}, f32[384,1152]{1,0:T(8,128)}, f32[384,384]{1,0:T(8,128)}, f32[384,384]{1,0:T(8,128)}, f32[384,1536]{1,0:T(8,128)}, /*index=5*/f32[1536,384]{1,0:T(8,128)}) custom-call(bf16[6144,384]{1,0:T(8,128)(2,1)} %get-tuple-element.91.big), custom_call_target="tpu_custom_call" | custom-call | tf_op jit(solution)/shard_map/unpack/pallas_call | solution.py:587
  215.4 2.7 %last_norm.1 = bf16[288,384]{1,0:T(8,128)(2,1)} custom-call(bf16[288,384]{1,0:T(8,128)(2,1)} %bitcast.22, f32[1,384]{1,0:T(1,128)} %reshape.118.gain, bf16[384,384]{1,0:T(8,128)(2,1)} %bitcast.37, bf16[384,384]{1,0:T(8,128)(2,1)} %bitcast.38, bf16[288,384]{1,0:T(8,128)(2,1)} %constant.23.clone.pdt, bf16[288,384]{1,0:T(8,128)(2,1)} %constant.24.clone.ptt, ...), custom_call_target="tpu_custom_call" | custom-call | tf_op jit(solution)/shard_map/last_norm/pallas_call | solution.py:841
  (26 shorter events, 0.8 us)
Async XLA Ops:
  30.5 18.6 %copy-start.7 = (f32[384]{0:T(512)S(1)}, f32[384]{0:T(512)}, u32[]{:S(2)}) copy-start(f32[384]{0:T(512)} %param.26) | copy-start | bytes 4612
  30.5 19.2 %copy-start.2 = (f32[3,3,3,1536]{3,2,1,0:T(4,128)S(1)}, f32[3,3,3,1536]{3,2,1,0:T(4,128)}, u32[]{:S(2)}) copy-start(f32[3,3,3,1536]{3,2,1,0:T(4,128)} %param.28) | copy-start | bytes 497668
  44.8 5.7 %collective-permute-start.1 = (bf16[144,384]{1,0:T(8,128)(2,1)S(1)}, bf16[144,384]{1,0:T(8,128)(2,1)S(1)}, u32[]{:S(2)}, u32[]{:S(2)}) collective-permute-start(bf16[144,384]{1,0:T(8,128)(2,1)S(1)} %get-tuple-element.105), channel_id=1, source_target_pairs={{4,0},{8,4},{12,8},{16,12},{20,16},{24,20},{28,24},{5,1},{9,5},{13... | collective-permute-start | bytes 331784 | tf_op jit(solution)/shard_map/ppermute | solution.py:701
  46.1 4.4 %collective-permute-start = (bf16[144,384]{1,0:T(8,128)(2,1)S(1)}, bf16[144,384]{1,0:T(8,128)(2,1)S(1)}, u32[]{:S(2)}, u32[]{:S(2)}) collective-permute-start(bf16[144,384]{1,0:T(8,128)(2,1)S(1)} %get-tuple-element.106), channel_id=1, source_target_pairs={{0,4},{4,8},{8,12},{12,16},{16,20},{20,24},{24,28},{1,5},{5,9},{9,... | collective-permute-start | bytes 331784 | tf_op jit(solution)/shard_map/ppermute | solution.py:700
  50.5 0.6 copy-start.4
  50.5 0.7 copy-start.5
  67.5 6.1 %copy-start.3 = (f32[27,1536]{1,0:T(8,128)S(1)}, f32[27,1536]{1,0:T(8,128)}, u32[]{:S(2)}) copy-start(f32[27,1536]{1,0:T(8,128)} %get-tuple-element.81) | copy-start | bytes 497668
  68.8 4.9 %collective-permute-start.3 = (bf16[144,1536]{1,0:T(8,128)(2,1)S(1)}, bf16[144,1536]{1,0:T(8,128)(2,1)S(1)}, u32[]{:S(2)}, u32[]{:S(2)}) collective-permute-start(bf16[144,1536]{1,0:T(8,128)(2,1)S(1)} %get-tuple-element.101), channel_id=1, source_target_pairs={{4,0},{8,4},{12,8},{16,12},{20,16},{24,20},{28,24},{5,1},{9,5},{13... | collective-permute-start | bytes 1327112 | tf_op jit(solution)/shard_map/ppermute | solution.py:750
  70.1 4.9 %collective-permute-start.2 = (bf16[144,1536]{1,0:T(8,128)(2,1)S(1)}, bf16[144,1536]{1,0:T(8,128)(2,1)S(1)}, u32[]{:S(2)}, u32[]{:S(2)}) collective-permute-start(bf16[144,1536]{1,0:T(8,128)(2,1)S(1)} %get-tuple-element.102), channel_id=1, source_target_pairs={{0,4},{4,8},{8,12},{12,16},{16,20},{20,24},{24,28},{1,5},{5,9},{9,... | collective-permute-start | bytes 1327112 | tf_op jit(solution)/shard_map/ppermute | solution.py:749
  73.6 1.3 copy-start
  75.0 0.8 copy-start.1
  109.0 23.7 %copy-start.6 = (f32[384]{0:T(512)S(1)}, f32[384]{0:T(512)}, u32[]{:S(2)}) copy-start(f32[384]{0:T(512)} %param.21) | copy-start | bytes 4612
  109.0 23.7 %copy-start.8 = (f32[1,384]{1,0:T(1,128)S(1)}, f32[1,384]{1,0:T(1,128)}, u32[]{:S(2)}) copy-start(f32[1,384]{1,0:T(1,128)} %get-tuple-element.83) | copy-start | bytes 4612
